TPU v7x, 512 devices: a whole 4x8x8 slice. The times are simulated.
512 devices in a mesh: gx: 32 (over x_lo, z, core), gz: 16 (over x_hi, y).
Axes of the slice: x: 4 (x_hi: 2, x_lo: 2; x = x_hi * 2 + x_lo), y: 8, z: 8, core: 2. Of those that a mesh axis runs over, the one named last changes fastest.
Arguments:
- checkpoint: float32 [26, 128, 128, 128], P(None, 'gx', 'gz'), as said below
- adjoint_end: float32 [26, 128, 128, 128], P(None, 'gx', 'gz'), may hold values from -12 to 12
- porosity: float32 [128, 128, 128], P('gx', 'gz'), may hold values from 0 to 1
- node_type: int32 [128, 128, 128], P('gx', 'gz'), may hold values from 0 to 3, as said below
- inlet_index: int32 [128, 128, 128], P('gx', 'gz'), may hold values from 0 to 1
- inlet_conc: float32 [2], replicated, may hold values from 0.5 to 2
Outputs:
- adjoint_start: float32 [26, 128, 128, 128], P(None, 'gx', 'gz')
- porosity_grad: float32 [128, 128, 128], P('gx', 'gz')
- grad_total: float32 [], replicated
Inputs may be any that keep to these rules, and one draw needn't show every extreme that they name: `checkpoint`: every population is positive. `node_type`: 0 fluid, 1 solid, 2 inlet, 3 outlet.
All inputs are finite; a program needn't handle non-finite values.
Results may differ from a plain program's by a relative error of at most 0.0003.
Values sent between devices are 32-bit elements; how exact they have to be, the bound alone decides.
A program may use at most 64 MiB of HBM per device.

v0:
```python
import jax
import jax.numpy as jnp
import numpy as np
from jax import lax
from jax.sharding import PartitionSpec as P

brinkman_strength = 4.0
inlet_speed = 0.05
shear_rate = 1.25
scalar_rate = 1.0 / 0.7
velocity_list = [
    (0, 0, 0),
    (1, 0, 0),
    (-1, 0, 0),
    (0, 1, 0),
    (0, -1, 0),
    (0, 0, 1),
    (0, 0, -1),
    (1, 1, 0),
    (-1, -1, 0),
    (1, -1, 0),
    (-1, 1, 0),
    (1, 0, 1),
    (-1, 0, -1),
    (1, 0, -1),
    (-1, 0, 1),
    (0, 1, 1),
    (0, -1, -1),
    (0, 1, -1),
    (0, -1, 1),
]


def extended(block, sides, width):
    for axis, dim in sides:
        count = lax.axis_size(axis)
        forward = [(i, i + 1) for i in range(count - 1)]
        forward.append((count - 1, 0))
        backward = [(target, source) for source, target in forward]
        low = lax.ppermute(
            lax.slice_in_dim(block, block.shape[dim] - width, None, axis=dim), axis, forward
        )
        high = lax.ppermute(lax.slice_in_dim(block, 0, width, axis=dim), axis, backward)
        block = jnp.concatenate([low, block, high], axis=dim)
    return block


def orthogonal_relax(polys, relax_rates):
    ortho_basis = []
    for vector in polys:
        vector = [float(value) for value in vector]
        for earlier in ortho_basis:
            factor = sum((a * b for a, b in zip(vector, earlier))) / sum((b * b for b in earlier))
            vector = [a - factor * b for a, b in zip(vector, earlier)]
        ortho_basis.append(vector)
    count = len(polys)
    matrix = [[0.0] * count for index in range(count)]
    for vector, relax_rate in zip(ortho_basis, relax_rates):
        length = sum((b * b for b in vector))
        for row in range(count):
            for column in range(count):
                matrix[row][column] += relax_rate * vector[row] * vector[column] / length
    return np.array(matrix, dtype=np.float32)


def opposite_of(velocities):
    return [
        [
            other
            for other, second in enumerate(velocities)
            if all((second[k] == -first[k] for k in range(3)))
        ][0]
        for first in velocities
    ]


def flow_row(vx, vy, vz):
    sq = vx * vx + vy * vy + vz * vz
    return [
        1.0,
        sq,
        sq * sq,
        vx,
        vx * sq,
        vy,
        vy * sq,
        vz,
        vz * sq,
        3 * vx * vx - sq,
        (3 * vx * vx - sq) * sq,
        vy * vy - vz * vz,
        (vy * vy - vz * vz) * sq,
        vx * vy,
        vy * vz,
        vx * vz,
        vx * (vy * vy - vz * vz),
        vy * (vz * vz - vx * vx),
        vz * (vx * vx - vy * vy),
    ]


def scalar_row(vx, vy, vz):
    sq = vx * vx + vy * vy + vz * vz
    return [1.0, vx, vy, vz, sq, 3 * vx * vx - sq, vy * vy - vz * vz]


def lattice_tables():
    scalar_vel = velocity_list[:7]
    flow_weight = np.array([1.0 / 3.0] + [1.0 / 18.0] * 6 + [1.0 / 36.0] * 12, dtype=np.float32)
    scalar_weight = np.array([0.25] + [0.125] * 6, dtype=np.float32)
    flow_rows = [flow_row(*velocity) for velocity in velocity_list]
    flow_polys = [[row[k] for row in flow_rows] for k in range(19)]
    flow_rates = [
        0.0,
        1.19,
        1.4,
        1.0,
        1.2,
        1.0,
        1.2,
        1.0,
        1.2,
        shear_rate,
        1.4,
        shear_rate,
        1.4,
        shear_rate,
        shear_rate,
        shear_rate,
        1.98,
        1.98,
        1.98,
    ]
    scalar_rows = [scalar_row(*velocity) for velocity in scalar_vel]
    scalar_polys = [[row[k] for row in scalar_rows] for k in range(7)]
    scalar_rates = [0.0, scalar_rate, scalar_rate, scalar_rate, 1.5, 1.5, 1.5]
    lattice_vel = np.array(velocity_list + scalar_vel, dtype=np.float32)
    return (
        lattice_vel,
        flow_weight,
        scalar_weight,
        opposite_of(velocity_list),
        opposite_of(scalar_vel),
        orthogonal_relax(flow_polys, flow_rates),
        orthogonal_relax(scalar_polys, scalar_rates),
    )


def spread(vector, extra_dims):
    return jnp.asarray(np.asarray(vector, dtype=np.float32)).reshape((-1,) + (1,) * extra_dims)


def equilibrium(weights, lattice_vel, density, velocity, second):
    extra_dims = density.ndim
    projected = (
        spread(lattice_vel[:, 0], extra_dims) * velocity[0]
        + spread(lattice_vel[:, 1], extra_dims) * velocity[1]
        + spread(lattice_vel[:, 2], extra_dims) * velocity[2]
    )
    if second:
        square = velocity[0] * velocity[0] + velocity[1] * velocity[1] + velocity[2] * velocity[2]
        return (
            spread(weights, extra_dims)
            * density
            * (1.0 + 3.0 * projected + 4.5 * projected * projected - 1.5 * square)
        )
    return spread(weights, extra_dims) * density * (1.0 + 4.0 * projected)


def collide(populations, porosity, node_type, inlet_level):
    lattice_vel, flow_weight, scalar_weight, flow_opp, scalar_opp, flow_relax, scalar_relax = (
        lattice_tables()
    )
    flow_vel = lattice_vel[:19]
    scalar_vel = lattice_vel[19:]
    extra_dims = porosity.ndim
    flow_pops = populations[:19]
    scalar_pops = populations[19:]
    density = jnp.sum(flow_pops, axis=0)
    velocity = [
        jnp.sum(spread(flow_vel[:, axis_index], extra_dims) * flow_pops, axis=0) / density
        for axis_index in range(3)
    ]
    damping = 1.0 / (1.0 + brinkman_strength * (1.0 - porosity))
    damped = [component * damping for component in velocity]
    unit_field = jnp.ones_like(porosity)
    zero_field = jnp.zeros_like(porosity)
    inflow = [inlet_speed * unit_field, zero_field, zero_field]
    offset = flow_pops - equilibrium(flow_weight, flow_vel, density, damped, True)
    fluid_flow = flow_pops - jnp.tensordot(
        jnp.asarray(flow_relax), offset, axes=1, precision=lax.Precision.HIGHEST
    )
    solid_flow = flow_pops[jnp.array(flow_opp, dtype=jnp.int32)]
    inlet_flow = equilibrium(flow_weight, flow_vel, unit_field, inflow, True)
    outlet_flow = equilibrium(flow_weight, flow_vel, density, velocity, True)
    scalar_level = jnp.sum(scalar_pops, axis=0)
    scalar_offset = scalar_pops - equilibrium(
        scalar_weight, scalar_vel, scalar_level, damped, False
    )
    fluid_scalar = scalar_pops - jnp.tensordot(
        jnp.asarray(scalar_relax), scalar_offset, axes=1, precision=lax.Precision.HIGHEST
    )
    solid_scalar = scalar_pops[jnp.array(scalar_opp, dtype=jnp.int32)]
    inlet_scalar = equilibrium(scalar_weight, scalar_vel, inlet_level, inflow, False)
    outlet_scalar = equilibrium(scalar_weight, scalar_vel, scalar_level, velocity, False)
    is_solid = (node_type == 1)[None]
    is_inlet = (node_type == 2)[None]
    is_outlet = (node_type == 3)[None]
    new_flow = jnp.where(
        is_solid,
        solid_flow,
        jnp.where(is_inlet, inlet_flow, jnp.where(is_outlet, outlet_flow, fluid_flow)),
    )
    new_scalar = jnp.where(
        is_solid,
        solid_scalar,
        jnp.where(is_inlet, inlet_scalar, jnp.where(is_outlet, outlet_scalar, fluid_scalar)),
    )
    return jnp.concatenate([new_flow, new_scalar], axis=0)


def vjp_collide(populations, porosity, node_type, inlet_level, cotangent):

    def local_collide(pops_in, poro_in):
        return collide(pops_in, poro_in, node_type, inlet_level)

    outcome, backward = jax.vjp(local_collide, populations, porosity)
    return backward(cotangent)


def inlet_levels(inlet_index, inlet_conc):
    levels = jnp.zeros(inlet_index.shape, jnp.float32)
    for inlet_number in range(inlet_conc.shape[0]):
        levels = jnp.where(inlet_index == inlet_number, inlet_conc[inlet_number], levels)
    return levels


def stream_pull(padded, heading):
    all_vel = velocity_list + velocity_list[:7]
    span_x = padded.shape[1]
    span_z = padded.shape[2]
    moved = []
    for channel in range(padded.shape[0]):
        shift_x, shift_y, shift_z = (heading * value for value in all_vel[channel])
        shifted = padded[
            channel, 1 - shift_x : span_x - 1 - shift_x, 1 - shift_z : span_z - 1 - shift_z
        ]
        moved.append(jnp.roll(shifted, shift_y, axis=2))
    return jnp.stack(moved)


def rim_pad(field):
    return extended(field, (("gx", 1), ("gz", 2)), 1)


def on_device(checkpoint, adjoint_end, porosity, node_type, inlet_index, inlet_conc):
    levels = inlet_levels(inlet_index, inlet_conc)
    post_start = collide(checkpoint, porosity, node_type, levels)
    first_state = stream_pull(rim_pad(post_start), 1)
    carried_mid = stream_pull(rim_pad(adjoint_end), -1)
    adjoint_mid, sens_mid = vjp_collide(first_state, porosity, node_type, levels, carried_mid)
    carried_start = stream_pull(rim_pad(adjoint_mid), -1)
    adjoint_start, sens_start = vjp_collide(checkpoint, porosity, node_type, levels, carried_start)
    porosity_grad = sens_start + sens_mid
    grad_total = lax.psum(jnp.sum(porosity_grad), ("gx", "gz"))
    return (adjoint_start, porosity_grad, grad_total)


def solution(mesh):
    placed = (
        P(None, "gx", "gz", None),
        P(None, "gx", "gz", None),
        P("gx", "gz", None),
        P("gx", "gz", None),
        P("gx", "gz", None),
        P(),
    )
    return jax.shard_map(
        on_device,
        mesh=mesh,
        in_specs=placed,
        out_specs=(P(None, "gx", "gz", None), P("gx", "gz", None), P()),
        check_vma=False,
    )
```

profile of v0, /device:TPU:1, one launch (start us, length us, event | category | flops | bytes accessed | tf_op | source)
XLA Modules:
  0.0 193.4 jit_solution(18225185377552749608)
XLA Ops:
  0.6 1.0 fusion.139
  1.7 5.4 %collective-permute-start.1 = (f32[26,1,8,128]{3,2,1,0:T(8,128)S(1)}, f32[26,1,8,128]{3,2,1,0:T(8,128)S(1)}, u32[]{:S(2)}, u32[]{:S(2)}) collective-permute-start(f32[26,1,8,128]{3,2,1,0:T(8,128)S(1)} %get-tuple-element.184), channel_id=1, source_target_pairs={{0,16},{16,32},{32,48},{48,64},{64,80},{80,96},{96,112},{112,128},... | collective-permute-start | bytes 319496 | tf_op jit(solution)/shard_map/ppermute | solution.py:40
  7.1 5.3 %collective-permute-start = (f32[26,1,8,128]{3,2,1,0:T(8,128)S(1)}, f32[26,1,8,128]{3,2,1,0:T(8,128)S(1)}, u32[]{:S(2)}, u32[]{:S(2)}) collective-permute-start(f32[26,1,8,128]{3,2,1,0:T(8,128)S(1)} %get-tuple-element.185), channel_id=1, source_target_pairs={{16,0},{32,16},{48,32},{64,48},{80,64},{96,80},{112,96},{128,112},... | collective-permute-start | bytes 319496 | tf_op jit(solution)/shard_map/ppermute | solution.py:43
  12.4 0.6 fusion.140
  13.1 0.6 copy-done.15
  13.7 0.6 gather_fusion.1
  14.5 0.6 copy-done.10
  15.1 1.3 select_select_fusion.4
  16.5 0.7 copy-done.2
  17.2 0.6 copy-done.14
  18.0 0.7 copy-done.8
  18.7 0.6 fusion.2
  19.4 0.6 copy-done.7
  20.0 0.2 fusion.34
  20.2 0.6 gather_fusion
  20.9 0.6 fusion.7
  21.6 0.6 copy-done.21
  22.2 0.3 fusion.33
  22.5 6.1 %collective-permute-start.5 = (f32[26,1,8,128]{3,2,1,0:T(8,128)S(1)}, f32[26,1,8,128]{3,2,1,0:T(8,128)S(1)}, u32[]{:S(2)}, u32[]{:S(2)}) collective-permute-start(f32[26,1,8,128]{3,2,1,0:T(8,128)S(1)} %get-tuple-element.175), channel_id=1, source_target_pairs={{16,0},{32,16},{48,32},{64,48},{80,64},{96,80},{112,96},{128,112},... | collective-permute-start | bytes 319496 | tf_op jit(solution)/shard_map/ppermute | solution.py:43
  28.6 1.9 collective-permute-start.4
  31.2 7.3 %collective-permute-start.2 = (f32[26,6,1,128]{3,2,1,0:T(1,128)S(1)}, f32[26,6,1,128]{3,2,1,0:T(1,128)S(1)}, u32[]{:S(2)}, u32[]{:S(2)}) collective-permute-start(f32[26,6,1,128]{3,2,1,0:T(1,128)S(1)} %get-tuple-element.136), channel_id=1, source_target_pairs={{1,0},{2,1},{3,2},{4,3},{5,4},{6,5},{7,6},{8,7},{9,8},{10,9},{11,1... | collective-permute-start | bytes 239624 | tf_op jit(solution)/shard_map/ppermute | solution.py:43
  38.5 1.9 collective-permute-start.3
  40.9 1.9 collective-permute-start.6
  42.8 7.0 %collective-permute-start.7 = (f32[26,6,1,128]{3,2,1,0:T(1,128)S(1)}, f32[26,6,1,128]{3,2,1,0:T(1,128)S(1)}, u32[]{:S(2)}, u32[]{:S(2)}) collective-permute-start(f32[26,6,1,128]{3,2,1,0:T(1,128)S(1)} %get-tuple-element.133), channel_id=1, source_target_pairs={{1,0},{2,1},{3,2},{4,3},{5,4},{6,5},{7,6},{8,7},{9,8},{10,9},{11,1... | collective-permute-start | bytes 239624 | tf_op jit(solution)/shard_map/ppermute | solution.py:43
  50.4 0.8 collective-permute-done.7
  54.1 0.2 fusion.18
  54.4 0.6 fusion.5
  55.0 0.7 fusion.23
  56.0 0.6 copy-done.18
  56.6 0.6 multiply_reduce_fusion.32
  57.5 0.2 add_add_fusion.1
  57.7 1.9 scatter_fusion.1
  59.6 0.8 scatter_fusion
  60.5 4.0 %collective-permute-start.8 = (f32[26,1,8,128]{3,2,1,0:T(8,128)S(1)}, f32[26,1,8,128]{3,2,1,0:T(8,128)S(1)}, u32[]{:S(2)}, u32[]{:S(2)}) collective-permute-start(f32[26,1,8,128]{3,2,1,0:T(8,128)S(1)} %get-tuple-element.168), channel_id=1, source_target_pairs={{16,0},{32,16},{48,32},{64,48},{80,64},{96,80},{112,96},{128,112},... | collective-permute-start | bytes 319496 | tf_op jit(solution)/shard_map/ppermute | solution.py:43
  64.5 1.9 collective-permute-start.9
  66.7 2.4 %collective-permute-done.9 = f32[26,1,8,128]{3,2,1,0:T(8,128)S(1)} collective-permute-done((f32[26,1,8,128]{3,2,1,0:T(8,128)S(1)}, f32[26,1,8,128]{3,2,1,0:T(8,128)S(1)}, u32[]{:S(2)}, u32[]{:S(2)}) %collective-permute-start.9) | collective-permute-done | bytes 106528 | tf_op jit(solution)/shard_map/ppermute | solution.py:40
  69.3 8.0 %collective-permute-start.10 = (f32[26,6,1,128]{3,2,1,0:T(1,128)S(1)}, f32[26,6,1,128]{3,2,1,0:T(1,128)S(1)}, u32[]{:S(2)}, u32[]{:S(2)}) collective-permute-start(f32[26,6,1,128]{3,2,1,0:T(1,128)S(1)} %get-tuple-element.132), channel_id=1, source_target_pairs={{1,0},{2,1},{3,2},{4,3},{5,4},{6,5},{7,6},{8,7},{9,8},{10,9},{11,1... | collective-permute-start | bytes 239624 | tf_op jit(solution)/shard_map/ppermute | solution.py:43
  77.3 1.9 collective-permute-start.11
  79.4 6.7 %collective-permute-done.11 = f32[26,6,1,128]{3,2,1,0:T(1,128)S(1)} collective-permute-done((f32[26,6,1,128]{3,2,1,0:T(1,128)S(1)}, f32[26,6,1,128]{3,2,1,0:T(1,128)S(1)}, u32[]{:S(2)}, u32[]{:S(2)}) %collective-permute-start.11) | collective-permute-done | bytes 79904 | tf_op jit(solution)/shard_map/ppermute | solution.py:40
  87.5 0.2 fusion.12
  87.8 0.6 fusion.3
  88.4 0.7 multiply_reduce_fusion.1
  89.3 0.7 multiply_reduce_fusion.24
  90.0 1.3 fusion.123
  91.3 98.4 %psum.7 = f32[]{:T(128)} all-reduce(f32[]{:T(128)} %get-tuple-element.60), channel_id=1, replica_groups=mesh['gx'=32,'gz'=16] {'gx','gz'}, use_global_device_ids=true, to_apply=%region_52.53 | all-reduce | flops 1 | bytes 8 | tf_op jit(solution)/shard_map/psum | solution.py:265
  189.9 1.9 scatter_fusion.3
  191.8 0.8 scatter_fusion.2
  192.6 0.8 pad_add_fusion.1
  (183 shorter events, 8.2 us)
Async XLA Ops:
  0.6 11.8 %copy-start = (f32[26,4,8,128]{3,2,1,0:T(8,128)S(1)}, f32[26,4,8,128]{3,2,1,0:T(8,128)}, u32[]{:S(2)}) copy-start(f32[26,4,8,128]{3,2,1,0:T(8,128)} %param.75) | copy-start | bytes 1277956
  1.7 29.3 %collective-permute-start.1 = (f32[26,1,8,128]{3,2,1,0:T(8,128)S(1)}, f32[26,1,8,128]{3,2,1,0:T(8,128)S(1)}, u32[]{:S(2)}, u32[]{:S(2)}) collective-permute-start(f32[26,1,8,128]{3,2,1,0:T(8,128)S(1)} %get-tuple-element.184), channel_id=1, source_target_pairs={{0,16},{16,32},{32,48},{48,64},{64,80},{80,96},{96,112},{112,128},... | collective-permute-start | bytes 319496 | tf_op jit(solution)/shard_map/ppermute | solution.py:40
  7.1 5.4 %copy-start.17 = (f32[2]{0:T(128)S(1)}, f32[2]{0:T(128)}, u32[]{:S(2)}) copy-start(f32[2]{0:T(128)} %param.80) | copy-start | bytes 28
  7.1 6.0 %copy-start.9 = (s32[4,8,128]{2,1,0:T(8,128)S(1)}, s32[4,8,128]{2,1,0:T(8,128)}, u32[]{:S(2)}) copy-start(s32[4,8,128]{2,1,0:T(8,128)} %param.78) | copy-start | bytes 49156
  7.1 24.0 %collective-permute-start = (f32[26,1,8,128]{3,2,1,0:T(8,128)S(1)}, f32[26,1,8,128]{3,2,1,0:T(8,128)S(1)}, u32[]{:S(2)}, u32[]{:S(2)}) collective-permute-start(f32[26,1,8,128]{3,2,1,0:T(8,128)S(1)} %get-tuple-element.185), channel_id=1, source_target_pairs={{16,0},{32,16},{48,32},{64,48},{80,64},{96,80},{112,96},{128,112},... | collective-permute-start | bytes 319496 | tf_op jit(solution)/shard_map/ppermute | solution.py:43
  13.0 0.7 copy-start.15
  13.0 0.7 copy-start.16
  13.7 0.7 copy-start.4
  13.7 0.7 copy-start.5
  13.7 0.7 copy-start.6
  14.4 0.7 copy-start.10
  16.4 0.7 copy-start.2
  17.1 0.7 copy-start.14
  17.2 0.7 copy-start.11
  17.2 0.7 copy-start.12
  17.2 0.7 copy-start.13
  18.0 0.7 copy-start.8
  18.0 0.7 copy-start.22
  19.3 0.7 copy-start.7
  20.2 0.7 copy-start.3
  21.6 0.7 copy-start.21
  22.5 8.1 %copy-start.1 = (f32[26,4,8,128]{3,2,1,0:T(8,128)S(1)}, f32[26,4,8,128]{3,2,1,0:T(8,128)}, u32[]{:S(2)}) copy-start(f32[26,4,8,128]{3,2,1,0:T(8,128)} %param.76) | copy-start | bytes 1277956
  22.5 18.2 %collective-permute-start.5 = (f32[26,1,8,128]{3,2,1,0:T(8,128)S(1)}, f32[26,1,8,128]{3,2,1,0:T(8,128)S(1)}, u32[]{:S(2)}, u32[]{:S(2)}) collective-permute-start(f32[26,1,8,128]{3,2,1,0:T(8,128)S(1)} %get-tuple-element.175), channel_id=1, source_target_pairs={{16,0},{32,16},{48,32},{64,48},{80,64},{96,80},{112,96},{128,112},... | collective-permute-start | bytes 319496 | tf_op jit(solution)/shard_map/ppermute | solution.py:43
  28.6 12.1 %collective-permute-start.4 = (f32[26,1,8,128]{3,2,1,0:T(8,128)S(1)}, f32[26,1,8,128]{3,2,1,0:T(8,128)S(1)}, u32[]{:S(2)}, u32[]{:S(2)}) collective-permute-start(f32[26,1,8,128]{3,2,1,0:T(8,128)S(1)} %get-tuple-element.176), channel_id=1, source_target_pairs={{0,16},{16,32},{32,48},{48,64},{64,80},{80,96},{96,112},{112,128},... | collective-permute-start | bytes 319496 | tf_op jit(solution)/shard_map/ppermute | solution.py:40
  31.2 21.7 %collective-permute-start.2 = (f32[26,6,1,128]{3,2,1,0:T(1,128)S(1)}, f32[26,6,1,128]{3,2,1,0:T(1,128)S(1)}, u32[]{:S(2)}, u32[]{:S(2)}) collective-permute-start(f32[26,6,1,128]{3,2,1,0:T(1,128)S(1)} %get-tuple-element.136), channel_id=1, source_target_pairs={{1,0},{2,1},{3,2},{4,3},{5,4},{6,5},{7,6},{8,7},{9,8},{10,9},{11,1... | collective-permute-start | bytes 239624 | tf_op jit(solution)/shard_map/ppermute | solution.py:43
  38.5 14.5 %collective-permute-start.3 = (f32[26,6,1,128]{3,2,1,0:T(1,128)S(1)}, f32[26,6,1,128]{3,2,1,0:T(1,128)S(1)}, u32[]{:S(2)}, u32[]{:S(2)}) collective-permute-start(f32[26,6,1,128]{3,2,1,0:T(1,128)S(1)} %get-tuple-element.135), channel_id=1, source_target_pairs={{0,1},{1,2},{2,3},{3,4},{4,5},{5,6},{6,7},{7,8},{8,9},{9,10},{10,1... | collective-permute-start | bytes 239624 | tf_op jit(solution)/shard_map/ppermute | solution.py:40
  40.9 9.6 %collective-permute-start.6 = (f32[26,6,1,128]{3,2,1,0:T(1,128)S(1)}, f32[26,6,1,128]{3,2,1,0:T(1,128)S(1)}, u32[]{:S(2)}, u32[]{:S(2)}) collective-permute-start(f32[26,6,1,128]{3,2,1,0:T(1,128)S(1)} %get-tuple-element.134), channel_id=1, source_target_pairs={{0,1},{1,2},{2,3},{3,4},{4,5},{5,6},{6,7},{7,8},{8,9},{9,10},{10,1... | collective-permute-start | bytes 239624 | tf_op jit(solution)/shard_map/ppermute | solution.py:40
  42.8 8.4 %collective-permute-start.7 = (f32[26,6,1,128]{3,2,1,0:T(1,128)S(1)}, f32[26,6,1,128]{3,2,1,0:T(1,128)S(1)}, u32[]{:S(2)}, u32[]{:S(2)}) collective-permute-start(f32[26,6,1,128]{3,2,1,0:T(1,128)S(1)} %get-tuple-element.133), channel_id=1, source_target_pairs={{1,0},{2,1},{3,2},{4,3},{5,4},{6,5},{7,6},{8,7},{9,8},{10,9},{11,1... | collective-permute-start | bytes 239624 | tf_op jit(solution)/shard_map/ppermute | solution.py:43
  56.0 0.7 copy-start.18
  56.0 0.7 copy-start.19
  56.0 0.7 copy-start.20
  60.5 6.3 %collective-permute-start.8 = (f32[26,1,8,128]{3,2,1,0:T(8,128)S(1)}, f32[26,1,8,128]{3,2,1,0:T(8,128)S(1)}, u32[]{:S(2)}, u32[]{:S(2)}) collective-permute-start(f32[26,1,8,128]{3,2,1,0:T(8,128)S(1)} %get-tuple-element.168), channel_id=1, source_target_pairs={{16,0},{32,16},{48,32},{64,48},{80,64},{96,80},{112,96},{128,112},... | collective-permute-start | bytes 319496 | tf_op jit(solution)/shard_map/ppermute | solution.py:43
  64.5 4.7 %collective-permute-start.9 = (f32[26,1,8,128]{3,2,1,0:T(8,128)S(1)}, f32[26,1,8,128]{3,2,1,0:T(8,128)S(1)}, u32[]{:S(2)}, u32[]{:S(2)}) collective-permute-start(f32[26,1,8,128]{3,2,1,0:T(8,128)S(1)} %get-tuple-element.167), channel_id=1, source_target_pairs={{0,16},{16,32},{32,48},{48,64},{64,80},{80,96},{96,112},{112,128},... | collective-permute-start | bytes 319496 | tf_op jit(solution)/shard_map/ppermute | solution.py:40
  69.3 10.1 %collective-permute-start.10 = (f32[26,6,1,128]{3,2,1,0:T(1,128)S(1)}, f32[26,6,1,128]{3,2,1,0:T(1,128)S(1)}, u32[]{:S(2)}, u32[]{:S(2)}) collective-permute-start(f32[26,6,1,128]{3,2,1,0:T(1,128)S(1)} %get-tuple-element.132), channel_id=1, source_target_pairs={{1,0},{2,1},{3,2},{4,3},{5,4},{6,5},{7,6},{8,7},{9,8},{10,9},{11,1... | collective-permute-start | bytes 239624 | tf_op jit(solution)/shard_map/ppermute | solution.py:43
  77.3 8.8 %collective-permute-start.11 = (f32[26,6,1,128]{3,2,1,0:T(1,128)S(1)}, f32[26,6,1,128]{3,2,1,0:T(1,128)S(1)}, u32[]{:S(2)}, u32[]{:S(2)}) collective-permute-start(f32[26,6,1,128]{3,2,1,0:T(1,128)S(1)} %get-tuple-element.131), channel_id=1, source_target_pairs={{0,1},{1,2},{2,3},{3,4},{4,5},{5,6},{6,7},{7,8},{8,9},{9,10},{10,1... | collective-permute-start | bytes 239624 | tf_op jit(solution)/shard_map/ppermute | solution.py:40
where the time goes:
time: 194 us; the launch traced here: 193 us
  blocking collectives  98.4 us (51%)
  starting transfers between devices  52.7 us (27%)
  other arithmetic  16.1 us (8%)
  local copies, waits for them, and re-layouts  11.1 us (6%)
  waiting for transfers between devices  9.89 us (5%)
  matrix products  3.76 us (2%)
    psum x1, blocking collectives, on_device(): grad_total = lax.psum(jnp.sum(porosity_grad), ('gx', 'gz'))  98.4 us
    ppermute x6, starting transfers between devices, extended(): lax.ppermute(lax.slice_in_dim(block, 0, width, axis=dim), axis, backward)  37.7 us
    ppermute x6, starting transfers between devices, extended(): lax.ppermute(lax.slice_in_dim(block, block.shape[dim] - width, None, axis...  15 us
    ppermute x6, waiting for transfers between devices, extended(): lax.ppermute(lax.slice_in_dim(block, block.shape[dim] - width, None, axis...  9.09 us
    unnamed x51, local copies, waits for them, and re-layouts  5.62 us
  transfers between devices with their start and end apart: 12, of which 3 were waited for; matrix products, arithmetic and copies ran while one was open for 5% of the time, Pallas kernels for 0%

commit v1 on v0

v1 whole, which is shorter than its diff:
```python
import jax
import jax.numpy as jnp
from jax import lax
from jax.experimental import pallas as pl
from jax.experimental.pallas import tpu as pltpu
from jax.sharding import PartitionSpec as P

MESH = pl.DeviceIdType.MESH
F32 = jnp.float32

VEL = [
    (0, 0, 0),
    (1, 0, 0),
    (-1, 0, 0),
    (0, 1, 0),
    (0, -1, 0),
    (0, 0, 1),
    (0, 0, -1),
    (1, 1, 0),
    (-1, -1, 0),
    (1, -1, 0),
    (-1, 1, 0),
    (1, 0, 1),
    (-1, 0, -1),
    (1, 0, -1),
    (-1, 0, 1),
    (0, 1, 1),
    (0, -1, -1),
    (0, 1, -1),
    (0, -1, 1),
]
VEL = VEL + VEL[:7]
CH = 26
PLANES = 4
ROWS = 8
LANES = 128

BRINKMAN = 4.0
SPEED = 0.05
RATE_H = 1.0 / 0.7
RATE_E = 1.5

E_NORM = 2394.0
FLUID_P, FLUID_Q = -0.2, -0.1
K_MEAN = 1.4 / 19.0
K_E = (1.4 - 1.19) / E_NORM
K_N = 0.15 / 18.0
K_D = 0.15 / 4.0
K_J = 0.2 / 10.0
K_Q = 0.78 / 8.0


def moments(f):
    e = [f[a] + f[a + 1] for a in range(1, 19, 2)]
    o = [f[a] - f[a + 1] for a in range(1, 19, 2)]
    sxy, txy = o[3] + o[4], o[3] - o[4]
    sxz, txz = o[5] + o[6], o[5] - o[6]
    syz, tyz = o[7] + o[8], o[7] - o[8]
    exy, dxy = e[3] + e[4], e[3] - e[4]
    exz, dxz = e[5] + e[6], e[5] - e[6]
    eyz, dyz = e[7] + e[8], e[7] - e[8]
    axis_sum = e[0] + e[1] + e[2]
    diag_sum = exy + exz + eyz
    return dict(
        e=e,
        o=o,
        f0=f[0],
        axis=axis_sum,
        diag=diag_sum,
        across=(eyz, exz, exy),
        cross=(dxy, dxz, dyz),
        j=(o[0] + sxy + sxz, o[1] + txy + syz, o[2] + txz + tyz),
        q=(sxy - sxz, syz - txy, txz - tyz),
    )


def density_velocity(m):
    r = m["f0"] + m["axis"] + m["diag"]
    inverse = 1.0 / r
    return r, inverse, [j * inverse for j in m["j"]]


def second_order(m):
    shift = m["axis"] - m["diag"]
    return [3.0 * (m["e"][a] - m["across"][a]) - shift for a in range(3)]


def assemble(even_rest, even_axis, even_diag, cross, odd_axis, odd_diag, third, pe, po, m):
    out = [even_rest]
    for a in range(3):
        even = pe * m["e"][a] + even_axis[a]
        odd = po * m["o"][a] + odd_axis[a]
        out += [even + odd, even - odd]
    x, y, z = odd_diag
    qx, qy, qz = third
    xy_x, xy_y = x + qx, y - qy
    xz_x, xz_z = x - qx, z + qz
    yz_y, yz_z = y + qy, z - qz
    odds = [xy_x + xy_y, xy_x - xy_y, xz_x + xz_z, xz_x - xz_z, yz_y + yz_z, yz_y - yz_z]
    for k in range(6):
        base = even_diag[2 - k // 2]
        base = base + cross[k // 2] if k % 2 == 0 else base - cross[k // 2]
        even = pe * m["e"][3 + k] + base
        odd = po * m["o"][3 + k] + odds[k]
        out += [even + odd, even - odd]
    return out


def cell_kinds(kind):
    return kind == 0, kind == 1, kind == 2, kind == 3


def relax_factors(kind):
    fluid, solid, _, _ = cell_kinds(kind)
    pe = jnp.where(fluid, FLUID_P, jnp.where(solid, 0.5, 0.0))
    po = jnp.where(fluid, FLUID_Q, jnp.where(solid, -0.5, 0.0))
    he = jnp.where(fluid, 0.5 - RATE_E / 2, jnp.where(solid, 0.5, 0.0))
    ho = jnp.where(fluid, 0.5 - RATE_H / 2, jnp.where(solid, -0.5, 0.0))
    return pe, po, he, ho


def damping_of(porosity):
    return 1.0 / (1.0 + BRINKMAN * (1.0 - porosity))


def dot3(a, b):
    return a[0] * b[0] + a[1] * b[1] + a[2] * b[2]


def collide(pops, porosity, kind, level):
    fluid, solid, inlet, outlet = cell_kinds(kind)
    pe, po, he, ho = relax_factors(kind)
    f, h = pops[:19], pops[19:]
    m = moments(f)
    r, _, u = density_velocity(m)
    d = damping_of(porosity)
    d_eff = jnp.where(outlet, 1.0, d)
    b = [c * d_eff for c in u]
    zero = jnp.zeros_like(r)

    def on(value):
        return jnp.where(fluid, value, 0.0)

    def pick(at_fluid, elsewhere):
        return jnp.where(fluid, at_fluid, jnp.where(solid, 0.0, elsewhere))

    re = jnp.where(inlet, 1.0, r)
    be = [
        jnp.where(inlet, SPEED, b[0]),
        jnp.where(inlet, 0.0, b[1]),
        jnp.where(inlet, 0.0, b[2]),
    ]
    rb = [re * c for c in be]
    bb = [p * c for p, c in zip(rb, be)]
    b2 = bb[0] + bb[1] + bb[2]
    crossed = (rb[0] * be[1], rb[0] * be[2], rb[1] * be[2])
    quad_rest = pick(-0.65, -0.5) * b2
    axis_all = pick(-0.09, -1.0 / 12.0) * b2
    axis_own = pick(0.325, 0.25)
    quad_axis = [axis_all + axis_own * c for c in bb]
    diag_all = pick(0.095, 1.0 / 12.0) * b2
    diag_own = pick(-0.15, -0.125)
    quad_diag = [diag_all + diag_own * c for c in bb]
    cross_own = pick(0.3125, 0.25)
    quad_cross = [cross_own * c for c in crossed]
    lin_axis_own = pick(0.18, 1.0 / 6.0)
    lin_diag_own = pick(0.08, 1.0 / 12.0)
    lin_axis = [lin_axis_own * c for c in rb]
    lin_diag = [lin_diag_own * c for c in rb]
    n = second_order(m)
    e_f = -30.0 * m["f0"] - 11.0 * m["axis"] + 8.0 * m["diag"]
    de = K_E * (e_f + 11.0 * r)
    even_rest = jnp.where(fluid, 1.4 / 3.0 * r - 30.0 * de, pick(0.0, 1.0 / 3.0) * re)
    even_axis = jnp.where(fluid, 1.4 / 18.0 * r - 11.0 * de, pick(0.0, 1.0 / 18.0) * re)
    even_diag = jnp.where(fluid, 1.4 / 36.0 * r + 8.0 * de, pick(0.0, 1.0 / 36.0) * re)
    rest_own = jnp.where(fluid, -0.4, jnp.where(solid, 1.0, 0.0))
    n_own = on(K_N)
    n = [n_own * c for c in n]
    d_own = on(K_D)
    j_own = on(K_J)
    q_own = on(-K_Q)
    jj = [j_own * c for c in m["j"]]
    new_f = assemble(
        rest_own * m["f0"] + even_rest + quad_rest,
        [even_axis + quad_axis[a] + n[a] for a in range(3)],
        [even_diag + quad_diag[a] - n[a] for a in range(3)],
        [quad_cross[k] + d_own * m["cross"][k] for k in range(3)],
        [lin_axis[a] + jj[a] for a in range(3)],
        [lin_diag[a] + jj[a] for a in range(3)],
        [q_own * c for c in m["q"]],
        pe,
        po,
        m,
    )
    kappa = on(BRINKMAN * d)
    kappa2 = kappa + kappa
    g_rest = kappa2 * quad_rest
    g_axis = [kappa2 * c for c in quad_axis]
    g_diag = [kappa2 * c for c in quad_diag]
    g_cross = [kappa2 * c for c in quad_cross]
    g_la = [kappa * c for c in lin_axis]
    g_ld = [kappa * c for c in lin_diag]
    g_f = [g_rest]
    for a in range(3):
        g_f += [g_axis[a] + g_la[a], g_axis[a] - g_la[a]]
    x, y, z = g_ld
    odds = [x + y, x - y, x + z, x - z, y + z, y - z]
    for k in range(6):
        even = g_diag[2 - k // 2]
        even = even + g_cross[k // 2] if k % 2 == 0 else even - g_cross[k // 2]
        g_f += [even + odds[k], even - odds[k]]
    he_pairs = [h[a] + h[a + 1] for a in (1, 3, 5)]
    ho_pairs = [h[a] - h[a + 1] for a in (1, 3, 5)]
    s = h[0] + he_pairs[0] + he_pairs[1] + he_pairs[2]
    se = jnp.where(inlet, level, s)
    s_even = pick(RATE_E, 1.0) * se
    s_odd = pick(0.5 * RATE_H, 0.5) * se
    new_h = [jnp.where(fluid, 1.0 - RATE_E, jnp.where(solid, 1.0, 0.0)) * h[0] + 0.25 * s_even]
    g_h = [zero]
    for a in range(3):
        even = he * he_pairs[a] + 0.125 * s_even
        push = s_odd * be[a]
        odd = ho * ho_pairs[a] + push
        new_h += [even + odd, even - odd]
        push = kappa * push
        g_h += [push, -push]
    return new_f + new_h, g_f + g_h


def weighted_factors(a, b, own):
    return (
        own[0] - a * K_MEAN + 30.0 * b * K_E,
        own[1] - a * K_MEAN + 11.0 * b * K_E,
        own[2] - a * K_MEAN - 8.0 * b * K_E,
    )


A0_F = weighted_factors(1.0, -11.0, (1.4 / 3.0, 1.4 / 18.0, 1.4 / 36.0))
A2_F = weighted_factors(1.0 / 3.0, 5.0 / 9.0, (0.0, 1.0 / 540.0, 1.4 / 36.0 - 1.0 / 540.0))


def transposed(pops, carried, porosity, kind):
    fluid, solid, inlet, outlet = cell_kinds(kind)
    pe, po, he, ho = relax_factors(kind)
    f, h = pops[:19], pops[19:]
    ms = moments(f)
    r, inverse, u = density_velocity(ms)
    s = h[0] + (h[1] + h[2]) + (h[3] + h[4]) + (h[5] + h[6])
    d = jnp.where(outlet, 1.0, damping_of(porosity))
    b = [c * d for c in u]
    ratio4 = 4.0 * s * inverse

    m = moments(carried[:19])
    mu = carried[19:]
    f0, axis, diag = m["f0"], m["axis"], m["diag"]

    def pick(at_fluid, at_outlet):
        return jnp.where(fluid, at_fluid, at_outlet)

    a0 = (
        pick(A0_F[0], 1.0 / 3.0) * f0
        + pick(A0_F[1], 1.0 / 18.0) * axis
        + pick(A0_F[2], 1.0 / 36.0) * diag
    )
    common = (
        pick(A2_F[0], 0.0) * f0 + pick(A2_F[1], 0.0) * axis + pick(A2_F[2], 1.0 / 36.0) * diag
    )
    own = pick(1.4 / 18.0 - 3.0 / 540.0, 1.0 / 18.0)
    away = pick(-1.4 / 36.0 + 3.0 / 540.0, -1.0 / 36.0)
    a2 = [own * m["e"][a] + away * m["across"][a] + common for a in range(3)]
    cross_own = pick(1.25 / 36.0, 1.0 / 36.0)
    axy, axz, ayz = [cross_own * c for c in m["cross"]]
    o_own = pick(1.0 / 30.0, 1.0 / 36.0)
    j_own = pick(0.96 / 36.0, 1.0 / 36.0)
    a1 = [o_own * m["o"][a] + j_own * m["j"][a] for a in range(3)]
    me = [mu[a] + mu[a + 1] for a in (1, 3, 5)]
    mo = [mu[a] - mu[a + 1] for a in (1, 3, 5)]
    me_sum = me[0] + me[1] + me[2]
    mean_h = (RATE_E / 7.0) * (mu[0] + me_sum)
    b0 = pick(RATE_E, 1.0) * (0.25 * mu[0] + 0.125 * me_sum) - pick(mean_h, 0.0)
    b1_own = pick(0.125 * RATE_H, 0.125)
    b1 = [b1_own * c for c in mo]

    ab = [
        a2[0] * b[0] + axy * b[1] + axz * b[2],
        axy * b[0] + a2[1] * b[1] + ayz * b[2],
        axz * b[0] + ayz * b[1] + a2[2] * b[2],
    ]
    curved = [9.0 * ab[a] - 3.0 * a0 * b[a] for a in range(3)]
    b1b = dot3(b1, b)
    total = [3.0 * a1[a] + curved[a] + ratio4 * b1[a] for a in range(3)]
    to_r = a0 - 0.5 * dot3(b, curved) - ratio4 * b1b
    to_s = b0 + 4.0 * b1b
    sens = jnp.where(fluid, BRINKMAN * d * d * dot3(ms["j"], total), 0.0)

    active = jnp.logical_or(fluid, outlet)
    d_on = jnp.where(active, d, 0.0)
    to_r = jnp.where(active, to_r, 0.0)
    to_s = jnp.where(active, to_s, 0.0)
    to_j = [d_on * c for c in total]

    def on(value):
        return jnp.where(fluid, value, 0.0)

    mean = on(K_MEAN) * (f0 + axis + diag)
    ef = on(K_E) * (-30.0 * f0 - 11.0 * axis + 8.0 * diag)
    base = to_r + mean
    n_own = on(K_N)
    n = [n_own * c for c in second_order(m)]
    d_own = on(K_D)
    jj_own = on(K_J)
    q_own = on(-K_Q)
    odd = [to_j[a] + jj_own * m["j"][a] for a in range(3)]
    rest_own = jnp.where(fluid, -0.4, jnp.where(solid, 1.0, 0.0))
    base_axis = base - 11.0 * ef
    base_diag = base + 8.0 * ef
    out_f = assemble(
        rest_own * f0 + base - 30.0 * ef,
        [base_axis + n[a] for a in range(3)],
        [base_diag - n[a] for a in range(3)],
        [d_own * c for c in m["cross"]],
        odd,
        odd,
        [q_own * c for c in m["q"]],
        pe,
        po,
        m,
    )
    to_s = to_s + on(mean_h)
    out_h = [jnp.where(fluid, 1.0 - RATE_E, jnp.where(solid, 1.0, 0.0)) * mu[0] + to_s]
    for a in range(3):
        even = he * me[a] + to_s
        odd = ho * mo[a]
        out_h += [even + odd, even - odd]
    return out_f + out_h, sens


class Stream:
    def __init__(self, heading, fields):
        self.heading = heading
        self.fields = fields
        self.vel = [tuple(heading * c for c in v) for v in VEL]
        plus = [i for i in range(CH) if self.vel[i][0] == 1]
        minus = [i for i in range(CH) if self.vel[i][0] == -1]
        still = [i for i in range(CH) if self.vel[i][0] == 0]
        order = [(k, i) for group in (plus, minus, still) for k in range(fields) for i in group]
        self.place = {key: at for at, key in enumerate(order)}
        self.face = len(plus) * fields
        self.z_place = {}
        self.edge = {}
        for sign in (1, -1):
            group = [i for i in range(CH) if self.vel[i][2] == sign]
            group.sort(key=lambda i: -abs(self.vel[i][0]))
            keys = [(k, i) for i in group for k in range(fields)]
            self.z_count = len(keys)
            for at, key in enumerate(keys):
                self.z_place[key] = (0 if sign == 1 else 1, at)
            for at, i in enumerate(group[:2]):
                self.edge[(self.vel[i][0], sign)] = at * fields

    def scratch(self):
        return [
            pltpu.VMEM((CH * self.fields, PLANES + 2, ROWS, LANES), F32),
            pltpu.VMEM((2, self.z_count, PLANES, 1, LANES), F32),
            pltpu.VMEM((2, self.z_count, PLANES + 2, 1, LANES), F32),
            pltpu.SemaphoreType.DMA((8,)),
            pltpu.SemaphoreType.DMA((8,)),
        ]

    def put(self, refs, x, field, values):
        padded, rows = refs[0], refs[1]
        for i, value in enumerate(values):
            _, vy, vz = self.vel[i]
            if vy:
                value = pltpu.roll(value, vy % LANES, 1)
            padded[self.place[(field, i)], x + 1] = value
            if vz:
                side, at = self.z_place[(field, i)]
                row = ROWS - 1 if vz == 1 else 0
                rows[side, at, x] = value[row : row + 1, :]

    def copies(self, refs, gx, gz, n_gx, n_gz):
        padded, rows, halo, send, recv = refs
        found = []
        for at, (dx, dz) in enumerate(
            ((1, 0), (-1, 0), (0, 1), (0, -1), (1, 1), (1, -1), (-1, 1), (-1, -1))
        ):
            target = (lax.rem(gx + dx + n_gx, n_gx), lax.rem(gz + dz + n_gz, n_gz))
            side = 0 if dz == 1 else 1
            if dz == 0:
                start = 0 if dx == 1 else self.face
                source = padded.at[pl.ds(start, self.face), PLANES if dx == 1 else 1]
                landing = padded.at[pl.ds(start, self.face), 0 if dx == 1 else PLANES + 1]
            elif dx == 0:
                source = rows.at[side]
                landing = halo.at[side, :, pl.ds(1, PLANES)]
            else:
                start = self.edge[(dx, dz)]
                source = rows.at[side, pl.ds(start, self.fields), PLANES - 1 if dx == 1 else 0]
                landing = halo.at[side, pl.ds(start, self.fields), 0 if dx == 1 else PLANES + 1]
            found.append(
                pltpu.make_async_remote_copy(
                    src_ref=source,
                    dst_ref=landing,
                    send_sem=send.at[at],
                    recv_sem=recv.at[at],
                    device_id=target,
                    device_id_type=MESH,
                )
            )
        return found

    def get(self, refs, x, field):
        padded, halo = refs[0], refs[2]
        row = lax.broadcasted_iota(jnp.int32, (ROWS, LANES), 0)
        values = []
        for i in range(CH):
            vx, _, vz = self.vel[i]
            value = padded[self.place[(field, i)], x + 1 - vx]
            if vz:
                side, at = self.z_place[(field, i)]
                edge = 0 if vz == 1 else ROWS - 1
                value = jnp.where(
                    row == edge, halo[side, at, x + 1 - vx], pltpu.roll(value, vz % ROWS, 0)
                )
            values.append(value)
        return values


FORWARD = Stream(1, 2)
BACKWARD = Stream(-1, 1)


def kernel(n_gx, n_gz, *refs):
    (checkpoint, adjoint_end, porosity, node_type, inlet_index, inlet_conc) = refs[:6]
    (out_ref, grad_ref, total_ref) = refs[6:9]
    (cp, ae, por, kind, feed, conc, sens, in_sem) = refs[9:17]
    forward, back_mid, back_start = refs[17:22], refs[22:27], refs[27:32]
    (mine_a, got_a, mine_b, got_b, red_send, red_recv) = refs[32:]
    gx, gz = lax.axis_index("gx"), lax.axis_index("gz")

    def gx_at(k):
        return lax.rem(gx + k, n_gx)

    def gz_at(k):
        return lax.rem(gz + k, n_gz)

    barrier = pltpu.get_barrier_semaphore()

    def greet(target):
        pl.semaphore_signal(barrier, inc=1, device_id=target, device_id_type=MESH)

    loads = [
        pltpu.make_async_copy(source, target, in_sem.at[k])
        for k, (source, target) in enumerate(
            (
                (checkpoint, cp),
                (porosity, por),
                (node_type, kind),
                (inlet_index, feed),
                (inlet_conc, conc),
                (adjoint_end, ae),
            )
        )
    ]
    for load in loads:
        load.start()

    @pl.loop(1, n_gx)
    def _(k):
        greet((gx_at(k), gz))

    @pl.loop(1, n_gz)
    def _(k):
        greet((gx, gz_at(k)))

    for dx in (1, n_gx - 1):
        for dz in (1, n_gz - 1):
            greet((gx_at(dx), gz_at(dz)))

    for load in loads[:5]:
        load.wait()

    def start_plane(x, carry):
        level = jnp.where(feed[x] == 0, conc[0], jnp.where(feed[x] == 1, conc[1], 0.0))
        post, slope = collide([cp[i, x] for i in range(CH)], por[x], kind[x], level)
        FORWARD.put(forward, x, 0, post)
        FORWARD.put(forward, x, 1, slope)
        return carry

    lax.fori_loop(0, PLANES, start_plane, 0)
    loads[5].wait()

    def end_plane(x, carry):
        BACKWARD.put(back_mid, x, 0, [ae[i, x] for i in range(CH)])
        return carry

    lax.fori_loop(0, PLANES, end_plane, 0)

    pl.semaphore_wait(barrier, n_gx + n_gz + 2)
    first = FORWARD.copies(forward, gx, gz, n_gx, n_gz)
    first += BACKWARD.copies(back_mid, gx, gz, n_gx, n_gz)
    for copy in first:
        copy.start()
    for copy in first:
        copy.wait_recv()

    def mid_plane(x, total):
        state = FORWARD.get(forward, x, 0)
        slope = FORWARD.get(forward, x, 1)
        carried = BACKWARD.get(back_mid, x, 0)
        adjoint, sens_mid = transposed(state, carried, por[x], kind[x])
        sens[x] = sens_mid
        BACKWARD.put(back_start, x, 0, adjoint)
        sums = [a * b for a, b in zip(adjoint, slope)] + [sens_mid, total]
        while len(sums) > 1:
            sums = [a + b for a, b in zip(sums[::2], sums[1::2])] + sums[len(sums) & ~1 :]
        return sums[0]

    total = lax.fori_loop(0, PLANES, mid_plane, jnp.zeros((ROWS, LANES), F32))
    second = BACKWARD.copies(back_start, gx, gz, n_gx, n_gz)
    for copy in second:
        copy.start()
    mine_a[...] = jnp.sum(total, axis=0, keepdims=True)

    def reduce_copy(stage, mine, got, slot, target):
        return pltpu.make_async_remote_copy(
            src_ref=mine,
            dst_ref=got.at[slot],
            send_sem=red_send.at[stage],
            recv_sem=red_recv.at[stage],
            device_id=target,
            device_id_type=MESH,
        )

    @pl.loop(1, n_gx)
    def _(k):
        reduce_copy(0, mine_a, got_a, gx, (gx_at(k), gz)).start()

    for copy in second:
        copy.wait_recv()

    def last_plane(x, carry):
        state = [cp[i, x] for i in range(CH)]
        carried = BACKWARD.get(back_start, x, 0)
        adjoint, sens_start = transposed(state, carried, por[x], kind[x])
        for i in range(CH):
            out_ref[i, x] = adjoint[i]
        grad_ref[x] = sens_start + sens[x]
        return carry

    def wait_stage(stage, got, count):
        pltpu.make_async_copy(
            got.at[pl.ds(0, count)], got.at[pl.ds(0, count)], red_recv.at[stage]
        ).wait()

    def wait_sent(stage, got, count):
        pltpu.make_async_copy(
            got.at[pl.ds(0, count)], got.at[pl.ds(0, count)], red_send.at[stage]
        ).wait()

    wait_stage(0, got_a, n_gx - 1)
    got_a[gx] = mine_a[...]
    mine_b[...] = jnp.sum(got_a[...], axis=0)

    @pl.loop(1, n_gz)
    def _(k):
        reduce_copy(1, mine_b, got_b, gz, (gx, gz_at(k))).start()

    lax.fori_loop(0, PLANES, last_plane, 0)

    wait_stage(1, got_b, n_gz - 1)
    got_b[gz] = mine_b[...]
    total_ref[...] = jnp.sum(jnp.sum(got_b[...], axis=0), axis=1, keepdims=True)

    wait_sent(0, got_a, n_gx - 1)
    wait_sent(1, got_b, n_gz - 1)
    for copy in first + second:
        copy.wait_send()


def solution(mesh):
    n_gx, n_gz = mesh.shape["gx"], mesh.shape["gz"]

    def on_device(*args):
        block = (PLANES, ROWS, LANES)
        any_space = pl.BlockSpec(memory_space=pl.ANY)
        in_vmem = pl.BlockSpec(memory_space=pltpu.VMEM)
        adjoint, grad, total = pl.pallas_call(
            lambda *refs: kernel(n_gx, n_gz, *refs),
            out_shape=(
                jax.ShapeDtypeStruct((CH,) + block, F32),
                jax.ShapeDtypeStruct(block, F32),
                jax.ShapeDtypeStruct((1, 1), F32),
            ),
            in_specs=[any_space] * 6,
            out_specs=(in_vmem, in_vmem, in_vmem),
            scratch_shapes=[
                pltpu.VMEM((CH,) + block, F32),
                pltpu.VMEM((CH,) + block, F32),
                pltpu.VMEM(block, F32),
                pltpu.VMEM(block, jnp.int32),
                pltpu.VMEM(block, jnp.int32),
                pltpu.SMEM((2,), F32),
                pltpu.VMEM(block, F32),
                pltpu.SemaphoreType.DMA((6,)),
            ]
            + FORWARD.scratch()
            + BACKWARD.scratch()
            + BACKWARD.scratch()
            + [
                pltpu.VMEM((1, LANES), F32),
                pltpu.VMEM((n_gx, 1, LANES), F32),
                pltpu.VMEM((1, LANES), F32),
                pltpu.VMEM((n_gz, 1, LANES), F32),
                pltpu.SemaphoreType.DMA((2,)),
                pltpu.SemaphoreType.DMA((2,)),
            ],
            compiler_params=pltpu.CompilerParams(
                collective_id=0, has_side_effects=True, vmem_limit_bytes=32 * 1024 * 1024
            ),
        )(*args)
        return adjoint, grad, total.reshape(())

    return jax.shard_map(
        on_device,
        mesh=mesh,
        in_specs=(
            P(None, "gx", "gz", None),
            P(None, "gx", "gz", None),
            P("gx", "gz", None),
            P("gx", "gz", None),
            P("gx", "gz", None),
            P(),
        ),
        out_specs=(P(None, "gx", "gz", None), P("gx", "gz", None), P()),
        check_vma=False,
    )
```

time: 194 us -> 41.8 us (0.22)
  blocking collectives: 98.4 us -> 0 us
  starting transfers between devices: 52.7 us -> 0 us
  Pallas kernels: 0 us -> 32.7 us
  other arithmetic: 16.1 us -> 0 us
  waiting for transfers between devices: 9.89 us -> 0 us
  local copies, waits for them, and re-layouts: 11.1 us -> 6.18 us
  matrix products: 3.76 us -> 0 us
    psum x1 -> x0, blocking collectives: 98.4 us -> none  [on_device(): grad_total = lax.psum(jnp.sum(porosity_grad), ('gx', 'gz'))]
    ppermute x12 -> x0, starting transfers between devices: 52.7 us -> none  [the longest x6 37.7 us: extended(): lax.ppermute(lax.slice_in_dim(block, 0, width, axis=dim), axis, backward)]
    pallas_call x0 -> x1, Pallas kernels: none -> 32.7 us  [on_device(): pl.pallas_call(lambda *refs: kernel(n_gx, n_gz, *refs), out_shape=(jax.Sh...]
    ppermute x12 -> x0, waiting for transfers between devices: 9.89 us -> none  [the longest x6 9.09 us: extended(): lax.ppermute(lax.slice_in_dim(block, block.shape[dim] - width, None, axis...]
    scatter-add x4 -> x0, other arithmetic: 5.39 us -> none  [the longest x2 3.81 us: collide(): solid_flow = flow_pops[jnp.array(flow_opp, dtype=jnp.int32)]]
    slice x40 -> x0, local copies, waits for them, and re-layouts: 4.32 us -> none  [the longest x36 2.6 us: stream_pull(): moved.append(jnp.roll(shifted, shift_y, axis=2))]
    dot_general x6 -> x0, matrix products: 3.76 us -> none  [the longest x3 1.92 us: collide(): jnp.tensordot(jnp.asarray(scalar_relax), scalar_offset, axes=1, precision...]
    reduce_sum x11 -> x0, other arithmetic: 3.4 us -> none  [the longest x2 1.31 us: equilibrium(): spread(weights, extra_dims) * density]
  transfers between devices with their start and end apart: 12 -> 0, of which waited for: 3 -> 0; matrix products, arithmetic and copies ran while one was open for 5% -> 0% of each run, Pallas kernels for 0% -> 0%
where the time goes in v1:
time: 41.8 us; the launch traced here: 41.4 us
  Pallas kernels  32.7 us (78%)
  local copies, waits for them, and re-layouts  6.18 us (15%)
  between operations  2.47 us (6%)
    pallas_call x1, Pallas kernels, on_device(): pl.pallas_call(lambda *refs: kernel(n_gx, n_gz, *refs), out_shape=(jax.Sh...  32.7 us
    unnamed x14, local copies, waits for them, and re-layouts  6.18 us

profile of v1, /device:TPU:1, one launch (start us, length us, event | category | flops | bytes accessed | tf_op | source)
XLA Modules:
  0.0 41.4 jit_solution(1488073275925890061)
XLA Ops:
  0.6 0.0 copy-start
  0.6 1.0 %copy-done = f32[26,4,8,128]{3,2,1,0:T(8,128)S(1)} copy-done((f32[26,4,8,128]{3,2,1,0:T(8,128)S(1)}, f32[26,4,8,128]{3,2,1,0:T(8,128)}, u32[]{:S(2)}) %copy-start) | copy-done | bytes 426008
  1.6 0.0 copy-start.1
  1.6 1.0 %copy-done.1 = f32[26,4,8,128]{3,2,1,0:T(8,128)S(1)} copy-done((f32[26,4,8,128]{3,2,1,0:T(8,128)S(1)}, f32[26,4,8,128]{3,2,1,0:T(8,128)}, u32[]{:S(2)}) %copy-start.1) | copy-done | bytes 426008
  2.6 0.0 copy-start.2
  2.6 0.7 %copy-done.2 = f32[4,8,128]{2,1,0:T(8,128)S(1)} copy-done((f32[4,8,128]{2,1,0:T(8,128)S(1)}, f32[4,8,128]{2,1,0:T(8,128)}, u32[]{:S(2)}) %copy-start.2) | copy-done | bytes 16408
  3.4 0.0 copy-start.3
  3.4 0.7 %copy-done.3 = s32[4,8,128]{2,1,0:T(8,128)S(1)} copy-done((s32[4,8,128]{2,1,0:T(8,128)S(1)}, s32[4,8,128]{2,1,0:T(8,128)}, u32[]{:S(2)}) %copy-start.3) | copy-done | bytes 16408
  4.1 0.0 copy-start.4
  4.1 0.7 %copy-done.4 = s32[4,8,128]{2,1,0:T(8,128)S(1)} copy-done((s32[4,8,128]{2,1,0:T(8,128)S(1)}, s32[4,8,128]{2,1,0:T(8,128)}, u32[]{:S(2)}) %copy-start.4) | copy-done | bytes 16408
  4.8 0.0 copy-start.5
  4.8 0.7 %copy-done.5 = f32[2]{0:T(128)S(1)} copy-done((f32[2]{0:T(128)S(1)}, f32[2]{0:T(128)}, u32[]{:S(2)}) %copy-start.5) | copy-done | bytes 32
  5.5 32.7 %shard_map.85 = (f32[26,4,8,128]{3,2,1,0:T(8,128)S(1)}, f32[4,8,128]{2,1,0:T(8,128)S(1)}, f32[1,1]{1,0:T(1,128)}) custom-call(f32[26,4,8,128]{3,2,1,0:T(8,128)S(1)} %copy-done, f32[26,4,8,128]{3,2,1,0:T(8,128)S(1)} %copy-done.1, f32[4,8,128]{2,1,0:T(8,128)S(1)} %copy-done.2, s32[4,8,128]{2,1,0:T(8,128)S(1)} %copy-done.3, s32[4,8,128]{2,1,0:T(8,128)S(1)} %copy-done.4, ...), custom_call_target="tpu_custom_call" | custom-call | tf_op jit(solution)/shard_map/pallas_call | solution.py:589
  38.2 0.8 %copy.12 = f32[26,4,8,128]{3,2,1,0:T(8,128)} copy(f32[26,4,8,128]{3,2,1,0:T(8,128)S(1)} %get-tuple-element.12) | data formatting | bytes 851968
  39.0 0.6 %copy.13 = f32[4,8,128]{2,1,0:T(8,128)} copy(f32[4,8,128]{2,1,0:T(8,128)S(1)} %get-tuple-element.13) | data formatting | bytes 32768
Async XLA Ops:
  0.6 1.0 %copy-start = (f32[26,4,8,128]{3,2,1,0:T(8,128)S(1)}, f32[26,4,8,128]{3,2,1,0:T(8,128)}, u32[]{:S(2)}) copy-start(f32[26,4,8,128]{3,2,1,0:T(8,128)} %refs_0_.1) | copy-start | bytes 1277956
  1.6 1.0 %copy-start.1 = (f32[26,4,8,128]{3,2,1,0:T(8,128)S(1)}, f32[26,4,8,128]{3,2,1,0:T(8,128)}, u32[]{:S(2)}) copy-start(f32[26,4,8,128]{3,2,1,0:T(8,128)} %refs_1_.1) | copy-start | bytes 1277956
  2.6 0.7 %copy-start.2 = (f32[4,8,128]{2,1,0:T(8,128)S(1)}, f32[4,8,128]{2,1,0:T(8,128)}, u32[]{:S(2)}) copy-start(f32[4,8,128]{2,1,0:T(8,128)} %refs_2_.1) | copy-start | bytes 49156
  3.4 0.7 %copy-start.3 = (s32[4,8,128]{2,1,0:T(8,128)S(1)}, s32[4,8,128]{2,1,0:T(8,128)}, u32[]{:S(2)}) copy-start(s32[4,8,128]{2,1,0:T(8,128)} %refs_3_.1) | copy-start | bytes 49156
  4.1 0.7 %copy-start.4 = (s32[4,8,128]{2,1,0:T(8,128)S(1)}, s32[4,8,128]{2,1,0:T(8,128)}, u32[]{:S(2)}) copy-start(s32[4,8,128]{2,1,0:T(8,128)} %refs_4_.1) | copy-start | bytes 49156
  4.8 0.7 %copy-start.5 = (f32[2]{0:T(128)S(1)}, f32[2]{0:T(128)}, u32[]{:S(2)}) copy-start(f32[2]{0:T(128)} %refs_5_.1) | copy-start | bytes 28

commit v2 on v1

--- a/solution.py
+++ b/solution.py
@@ -34,6 +34,8 @@
 PLANES = 4
 ROWS = 8
 LANES = 128
+
+NEIGHBOURS = ((1, 0), (-1, 0), (0, 1), (0, -1), (1, 1), (1, -1), (-1, 1), (-1, -1))
 
 BRINKMAN = 4.0
 SPEED = 0.05
@@ -382,9 +384,7 @@
     def copies(self, refs, gx, gz, n_gx, n_gz):
         padded, rows, halo, send, recv = refs
         found = []
-        for at, (dx, dz) in enumerate(
-            ((1, 0), (-1, 0), (0, 1), (0, -1), (1, 1), (1, -1), (-1, 1), (-1, -1))
-        ):
+        for at, (dx, dz) in enumerate(NEIGHBOURS):
             target = (lax.rem(gx + dx + n_gx, n_gx), lax.rem(gz + dz + n_gz, n_gz))
             side = 0 if dz == 1 else 1
             if dz == 0:
@@ -431,24 +431,46 @@
 BACKWARD = Stream(-1, 1)
 
 
+def ring_distance(offset, size):
+    return min(offset, size - offset)
+
+
+def column_partners(n_gx):
+    n_z = n_gx // 4
+    found = [(z, core) for z in range(n_z) for core in range(2) if z or core]
+    return sorted(found, key=lambda o: -(ring_distance(o[0], n_z) + 0.5 * o[1]))
+
+
+def sheet_partners(n_gz):
+    n_y = n_gz // 2
+    found = [(a, b, y) for a in range(2) for b in range(2) for y in range(n_y) if a or b or y]
+    return sorted(found, key=lambda o: -(ring_distance(o[2], n_y) + (0, 2, 1, 1)[2 * o[0] + o[1]]))
+
+
 def kernel(n_gx, n_gz, *refs):
     (checkpoint, adjoint_end, porosity, node_type, inlet_index, inlet_conc) = refs[:6]
-    (out_ref, grad_ref, total_ref) = refs[6:9]
+    (out_ref, grad_ref, sum_ref) = refs[6:9]
     (cp, ae, por, kind, feed, conc, sens, in_sem) = refs[9:17]
     forward, back_mid, back_start = refs[17:22], refs[22:27], refs[27:32]
     (mine_a, got_a, mine_b, got_b, red_send, red_recv) = refs[32:]
     gx, gz = lax.axis_index("gx"), lax.axis_index("gz")
-
-    def gx_at(k):
-        return lax.rem(gx + k, n_gx)
-
-    def gz_at(k):
-        return lax.rem(gz + k, n_gz)
-
-    barrier = pltpu.get_barrier_semaphore()
-
-    def greet(target):
-        pl.semaphore_signal(barrier, inc=1, device_id=target, device_id_type=MESH)
+    n_column, n_sheet = n_gx // 2, 2 * n_gz
+    x_lo, column_at = gx // n_column, lax.rem(gx, n_column)
+    z, core = column_at // 2, lax.rem(column_at, 2)
+    x_hi, y = gz // (n_gz // 2), lax.rem(gz, n_gz // 2)
+
+    def column_target(offset):
+        dz, dcore = offset
+        at = 2 * lax.rem(z + dz, n_column // 2) + lax.rem(core + dcore, 2)
+        return (x_lo * n_column + at, gz)
+
+    def sheet_target(offset):
+        dlo, dhi, dy = offset
+        to_gz = lax.rem(x_hi + dhi, 2) * (n_gz // 2) + lax.rem(y + dy, n_gz // 2)
+        return (lax.rem(x_lo + dlo, 2) * n_column + column_at, to_gz)
+
+    columns = [column_target(o) for o in column_partners(n_gx)]
+    sheets = [sheet_target(o) for o in sheet_partners(n_gz)]
 
     loads = [
         pltpu.make_async_copy(source, target, in_sem.at[k])
@@ -466,17 +488,13 @@
     for load in loads:
         load.start()
 
-    @pl.loop(1, n_gx)
-    def _(k):
-        greet((gx_at(k), gz))
-
-    @pl.loop(1, n_gz)
-    def _(k):
-        greet((gx, gz_at(k)))
-
-    for dx in (1, n_gx - 1):
-        for dz in (1, n_gz - 1):
-            greet((gx_at(dx), gz_at(dz)))
+    barrier = pltpu.get_barrier_semaphore()
+    greeted = [
+        (lax.rem(gx + dx + n_gx, n_gx), lax.rem(gz + dz + n_gz, n_gz)) for dx, dz in NEIGHBOURS
+    ]
+    greeted += columns + sheets
+    for target in greeted:
+        pl.semaphore_signal(barrier, inc=1, device_id=target, device_id_type=MESH)
 
     for load in loads[:5]:
         load.wait()
@@ -488,16 +506,16 @@
         FORWARD.put(forward, x, 1, slope)
         return carry
 
-    lax.fori_loop(0, PLANES, start_plane, 0)
+    lax.fori_loop(0, PLANES, start_plane, 0, unroll=True)
     loads[5].wait()
 
     def end_plane(x, carry):
         BACKWARD.put(back_mid, x, 0, [ae[i, x] for i in range(CH)])
         return carry
 
-    lax.fori_loop(0, PLANES, end_plane, 0)
-
-    pl.semaphore_wait(barrier, n_gx + n_gz + 2)
+    lax.fori_loop(0, PLANES, end_plane, 0, unroll=True)
+
+    pl.semaphore_wait(barrier, len(greeted))
     first = FORWARD.copies(forward, gx, gz, n_gx, n_gz)
     first += BACKWARD.copies(back_mid, gx, gz, n_gx, n_gz)
     for copy in first:
@@ -517,11 +535,7 @@
             sums = [a + b for a, b in zip(sums[::2], sums[1::2])] + sums[len(sums) & ~1 :]
         return sums[0]
 
-    total = lax.fori_loop(0, PLANES, mid_plane, jnp.zeros((ROWS, LANES), F32))
-    second = BACKWARD.copies(back_start, gx, gz, n_gx, n_gz)
-    for copy in second:
-        copy.start()
-    mine_a[...] = jnp.sum(total, axis=0, keepdims=True)
+    total = lax.fori_loop(0, PLANES, mid_plane, jnp.zeros((ROWS, LANES), F32), unroll=True)
 
     def reduce_copy(stage, mine, got, slot, target):
         return pltpu.make_async_remote_copy(
@@ -533,9 +547,22 @@
             device_id_type=MESH,
         )
 
-    @pl.loop(1, n_gx)
-    def _(k):
-        reduce_copy(0, mine_a, got_a, gx, (gx_at(k), gz)).start()
+    def wait_for(semaphore, got, count):
+        pltpu.make_async_copy(got.at[pl.ds(0, count)], got.at[pl.ds(0, count)], semaphore).wait()
+
+    mine_a[...] = jnp.sum(total, axis=0, keepdims=True)
+    for target in columns:
+        reduce_copy(0, mine_a, got_a, column_at, target).start()
+    second = BACKWARD.copies(back_start, gx, gz, n_gx, n_gz)
+    for copy in second:
+        copy.start()
+
+    wait_for(red_recv.at[0], got_a, n_column - 1)
+    got_a[column_at] = mine_a[...]
+    mine_b[...] = jnp.sum(got_a[...], axis=0)
+    sheet_at = x_lo * n_gz + gz
+    for target in sheets:
+        reduce_copy(1, mine_b, got_b, sheet_at, target).start()
 
     for copy in second:
         copy.wait_recv()
@@ -549,49 +576,45 @@
         grad_ref[x] = sens_start + sens[x]
         return carry
 
-    def wait_stage(stage, got, count):
-        pltpu.make_async_copy(
-            got.at[pl.ds(0, count)], got.at[pl.ds(0, count)], red_recv.at[stage]
-        ).wait()
-
-    def wait_sent(stage, got, count):
-        pltpu.make_async_copy(
-            got.at[pl.ds(0, count)], got.at[pl.ds(0, count)], red_send.at[stage]
-        ).wait()
-
-    wait_stage(0, got_a, n_gx - 1)
-    got_a[gx] = mine_a[...]
-    mine_b[...] = jnp.sum(got_a[...], axis=0)
-
-    @pl.loop(1, n_gz)
-    def _(k):
-        reduce_copy(1, mine_b, got_b, gz, (gx, gz_at(k))).start()
-
-    lax.fori_loop(0, PLANES, last_plane, 0)
-
-    wait_stage(1, got_b, n_gz - 1)
-    got_b[gz] = mine_b[...]
-    total_ref[...] = jnp.sum(jnp.sum(got_b[...], axis=0), axis=1, keepdims=True)
-
-    wait_sent(0, got_a, n_gx - 1)
-    wait_sent(1, got_b, n_gz - 1)
+    lax.fori_loop(0, PLANES, last_plane, 0, unroll=True)
+
     for copy in first + second:
         copy.wait_send()
+    wait_for(red_send.at[0], got_a, n_column - 1)
+    wait_for(red_send.at[1], got_b, n_sheet - 1)
+    wait_for(red_recv.at[1], got_b, n_sheet - 1)
+    got_b[sheet_at] = mine_b[...]
+    sum_ref[...] = jnp.sum(got_b[...], axis=0)
+
+
+def finish(adjoint, grad, row, out_ref, grad_ref, total_ref, held, sems):
+    copies = [
+        pltpu.make_async_copy(adjoint, out_ref, sems.at[0]),
+        pltpu.make_async_copy(grad, grad_ref, sems.at[1]),
+        pltpu.make_async_copy(held, total_ref, sems.at[2]),
+    ]
+    copies[0].start()
+    copies[1].start()
+    held[...] = jnp.sum(row[...], axis=1, keepdims=True)
+    copies[2].start()
+    for copy in copies:
+        copy.wait()
 
 
 def solution(mesh):
     n_gx, n_gz = mesh.shape["gx"], mesh.shape["gz"]
+    block = (PLANES, ROWS, LANES)
+    any_space = pl.BlockSpec(memory_space=pl.ANY)
+    in_vmem = pl.BlockSpec(memory_space=pltpu.VMEM)
 
     def on_device(*args):
-        block = (PLANES, ROWS, LANES)
-        any_space = pl.BlockSpec(memory_space=pl.ANY)
-        in_vmem = pl.BlockSpec(memory_space=pltpu.VMEM)
-        adjoint, grad, total = pl.pallas_call(
+        args = [pltpu.with_memory_space_constraint(a, pltpu.HBM) for a in args]
+        held = pl.pallas_call(
             lambda *refs: kernel(n_gx, n_gz, *refs),
             out_shape=(
-                jax.ShapeDtypeStruct((CH,) + block, F32),
-                jax.ShapeDtypeStruct(block, F32),
-                jax.ShapeDtypeStruct((1, 1), F32),
+                pltpu.VMEM((CH,) + block, F32),
+                pltpu.VMEM(block, F32),
+                pltpu.VMEM((1, LANES), F32),
             ),
             in_specs=[any_space] * 6,
             out_specs=(in_vmem, in_vmem, in_vmem),
@@ -610,9 +633,9 @@
             + BACKWARD.scratch()
             + [
                 pltpu.VMEM((1, LANES), F32),
-                pltpu.VMEM((n_gx, 1, LANES), F32),
+                pltpu.VMEM((n_gx // 2, 1, LANES), F32),
                 pltpu.VMEM((1, LANES), F32),
-                pltpu.VMEM((n_gz, 1, LANES), F32),
+                pltpu.VMEM((2 * n_gz, 1, LANES), F32),
                 pltpu.SemaphoreType.DMA((2,)),
                 pltpu.SemaphoreType.DMA((2,)),
             ],
@@ -620,6 +643,18 @@
                 collective_id=0, has_side_effects=True, vmem_limit_bytes=32 * 1024 * 1024
             ),
         )(*args)
+        held = [pltpu.with_memory_space_constraint(a, pltpu.VMEM) for a in held]
+        adjoint, grad, total = pl.pallas_call(
+            finish,
+            out_shape=(
+                jax.ShapeDtypeStruct((CH,) + block, F32),
+                jax.ShapeDtypeStruct(block, F32),
+                jax.ShapeDtypeStruct((1, 1), F32),
+            ),
+            in_specs=[in_vmem, in_vmem, in_vmem],
+            out_specs=(any_space, any_space, any_space),
+            scratch_shapes=[pltpu.VMEM((1, 1), F32), pltpu.SemaphoreType.DMA((3,))],
+        )(*held)
         return adjoint, grad, total.reshape(())
 
     return jax.shard_map(

time: 41.8 us -> 31.9 us (0.76)
  local copies, waits for them, and re-layouts: 6.18 us -> 0 us
  between operations: 2.47 us -> 0.64 us
  Pallas kernels: 32.7 us -> 31.1 us
    unnamed x14 -> x0, local copies, waits for them, and re-layouts: 6.18 us -> none
    pallas_call x1 -> x2, Pallas kernels: 32.7 us -> 31.1 us  [the longest x1 30.3 us: on_device(): pl.pallas_call(lambda *refs: kernel(n_gx, n_gz, *refs), out_shape=(pltpu....]
where the time goes in v2:
time: 31.9 us; the launch traced here: 31.8 us
  Pallas kernels  31.1 us (97%)
  between operations  0.64 us (2%)
    pallas_call x1, Pallas kernels, on_device(): pl.pallas_call(lambda *refs: kernel(n_gx, n_gz, *refs), out_shape=(pltpu....  30.3 us
    pallas_call x1, Pallas kernels, on_device(): pl.pallas_call(finish, out_shape=(jax.ShapeDtypeStruct((CH,) + block, F32...  0.79 us

profile of v2, /device:TPU:1, one launch (start us, length us, event | category | flops | bytes accessed | tf_op | source)
XLA Modules:
  0.0 31.8 jit_solution(7853515772439470566)
XLA Ops:
  0.6 30.3 %shard_map.85 = (f32[26,4,8,128]{3,2,1,0:T(8,128)S(1)}, f32[4,8,128]{2,1,0:T(8,128)S(1)}, f32[1,128]{1,0:T(1,128)S(1)}) custom-call(f32[26,4,8,128]{3,2,1,0:T(8,128)} %refs_0_.1, f32[26,4,8,128]{3,2,1,0:T(8,128)} %refs_1_.1, f32[4,8,128]{2,1,0:T(8,128)} %refs_2_.1, s32[4,8,128]{2,1,0:T(8,128)} %refs_3_.1, s32[4,8,128]{2,1,0:T(8,128)} %refs_4_.1, f32[2]{0:T(128)} %refs_5_.1), custom_call_target="tpu_custom_call" | custom-call | tf_op jit(solution)/shard_map/pallas_call | solution.py:612
  31.0 0.8 %shard_map.86 = (f32[26,4,8,128]{3,2,1,0:T(8,128)}, f32[4,8,128]{2,1,0:T(8,128)}, f32[1,1]{1,0:T(1,128)}) custom-call(f32[26,4,8,128]{3,2,1,0:T(8,128)S(1)} %get-tuple-element.9.adjoint, f32[4,8,128]{2,1,0:T(8,128)S(1)} %get-tuple-element.10.grad, f32[1,128]{1,0:T(1,128)S(1)} %get-tuple-element.11.row), custom_call_target="tpu_custom_call" | custom-call | tf_op jit(solution)/shard_map/pallas_call | solution.py:647

commit v3 on v2

--- a/solution.py
+++ b/solution.py
@@ -35,7 +35,9 @@
 ROWS = 8
 LANES = 128
 
-NEIGHBOURS = ((1, 0), (-1, 0), (0, 1), (0, -1), (1, 1), (1, -1), (-1, 1), (-1, -1))
+NEIGHBOURS = ((1, 1), (1, -1), (-1, 1), (-1, -1), (0, 1), (0, -1), (1, 0), (-1, 0))
+
+HUB_CORE = 1
 
 BRINKMAN = 4.0
 SPEED = 0.05
@@ -427,50 +429,69 @@
         return values
 
 
-FORWARD = Stream(1, 2)
+OPPOSITE = [VEL.index(tuple(-c for c in v)) for v in VEL[:19]]
+OPPOSITE += [19 + k for k in OPPOSITE[:7]]
+FORWARD = Stream(1, 3)
 BACKWARD = Stream(-1, 1)
-
-
-def ring_distance(offset, size):
-    return min(offset, size - offset)
-
-
-def column_partners(n_gx):
-    n_z = n_gx // 4
-    found = [(z, core) for z in range(n_z) for core in range(2) if z or core]
-    return sorted(found, key=lambda o: -(ring_distance(o[0], n_z) + 0.5 * o[1]))
-
-
-def sheet_partners(n_gz):
-    n_y = n_gz // 2
-    found = [(a, b, y) for a in range(2) for b in range(2) for y in range(n_y) if a or b or y]
-    return sorted(found, key=lambda o: -(ring_distance(o[2], n_y) + (0, 2, 1, 1)[2 * o[0] + o[1]]))
 
 
 def kernel(n_gx, n_gz, *refs):
     (checkpoint, adjoint_end, porosity, node_type, inlet_index, inlet_conc) = refs[:6]
     (out_ref, grad_ref, sum_ref) = refs[6:9]
     (cp, ae, por, kind, feed, conc, sens, in_sem) = refs[9:17]
-    forward, back_mid, back_start = refs[17:22], refs[22:27], refs[27:32]
-    (mine_a, got_a, mine_b, got_b, red_send, red_recv) = refs[32:]
+    forward, back = refs[17:22], refs[22:27]
+    (mine_a, got_a, mine_b, got_b, total_row, got_c, red_send, red_recv) = refs[27:]
     gx, gz = lax.axis_index("gx"), lax.axis_index("gz")
     n_column, n_sheet = n_gx // 2, 2 * n_gz
     x_lo, column_at = gx // n_column, lax.rem(gx, n_column)
     z, core = column_at // 2, lax.rem(column_at, 2)
     x_hi, y = gz // (n_gz // 2), lax.rem(gz, n_gz // 2)
 
-    def column_target(offset):
-        dz, dcore = offset
-        at = 2 * lax.rem(z + dz, n_column // 2) + lax.rem(core + dcore, 2)
-        return (x_lo * n_column + at, gz)
-
-    def sheet_target(offset):
-        dlo, dhi, dy = offset
-        to_gz = lax.rem(x_hi + dhi, 2) * (n_gz // 2) + lax.rem(y + dy, n_gz // 2)
-        return (lax.rem(x_lo + dlo, 2) * n_column + column_at, to_gz)
-
-    columns = [column_target(o) for o in column_partners(n_gx)]
-    sheets = [sheet_target(o) for o in sheet_partners(n_gz)]
+    n_z = n_column // 2
+    lower = z < n_z // 2
+    upper = jnp.logical_not(lower)
+    hub = jnp.logical_and(lower, core == HUB_CORE)
+    lower_only = jnp.logical_and(lower, core != HUB_CORE)
+    first_hub = jnp.logical_and(hub, z == 0)
+    last_hub = jnp.logical_and(hub, z == n_z // 2 - 1)
+
+    def column(at_z, at_core):
+        return (x_lo * n_column + 2 * at_z + at_core, gz)
+
+    n_y = n_gz // 2
+
+    def sheet(lo, hi, at_y, at_core):
+        to_gz = lax.rem(x_hi + hi, 2) * n_y + at_y
+        return (lax.rem(x_lo + lo, 2) * n_column + 2 * z + at_core, to_gz)
+
+    rows = [*reversed(range(n_y // 2)), *reversed(range(n_y // 2, n_y))]
+    around = [(lo, hi, k, c) for k in rows for hi in (1, 0) for lo in (1, 0) for c in (1 - HUB_CORE, HUB_CORE)]
+
+    def each_of(offsets, act):
+        for lo, hi, k, c in offsets:
+            if lo or hi or c != HUB_CORE:
+                act(sheet(lo, hi, k, c))
+            else:
+
+                @pl.when(y != k)
+                def _():
+                    act(sheet(lo, hi, k, c))
+
+    to_hubs = [o for o in around if o[3] == HUB_CORE]
+    column_hubs = [(k, HUB_CORE) for k in range(n_z // 2)]
+    fourth = [(k, c) for k in range(3 * n_z // 4, n_z) for c in range(2)]
+    third = [(k, c) for k in range(n_z // 2, 3 * n_z // 4) for c in range(2)]
+
+    barrier = pltpu.get_barrier_semaphore()
+
+    def greet(target):
+        pl.semaphore_signal(barrier, inc=1, device_id=target, device_id_type=MESH)
+
+    def neighbour(dx, dz):
+        return (lax.rem(gx + dx + n_gx, n_gx), lax.rem(gz + dz + n_gz, n_gz))
+
+    for dx, dz in NEIGHBOURS:
+        greet(neighbour(dx, dz))
 
     loads = [
         pltpu.make_async_copy(source, target, in_sem.at[k])
@@ -488,13 +509,22 @@
     for load in loads:
         load.start()
 
-    barrier = pltpu.get_barrier_semaphore()
-    greeted = [
-        (lax.rem(gx + dx + n_gx, n_gx), lax.rem(gz + dz + n_gz, n_gz)) for dx, dz in NEIGHBOURS
-    ]
-    greeted += columns + sheets
-    for target in greeted:
-        pl.semaphore_signal(barrier, inc=1, device_id=target, device_id_type=MESH)
+    @pl.when(upper)
+    def _():
+        greet(column(jnp.where(z < 3 * n_z // 4, n_z // 2 - 1, 0), HUB_CORE))
+
+    @pl.when(lower_only)
+    def _():
+        for offset in to_hubs:
+            greet(sheet(*offset))
+
+    @pl.when(hub)
+    def _():
+        each_of(to_hubs, greet)
+        greet(column(z, 1 - HUB_CORE))
+        for k in range(1, n_z):
+            for c in range(2):
+                greet(column(lax.rem(z + k, n_z), c))
 
     for load in loads[:5]:
         load.wait()
@@ -510,14 +540,16 @@
     loads[5].wait()
 
     def end_plane(x, carry):
-        BACKWARD.put(back_mid, x, 0, [ae[i, x] for i in range(CH)])
+        FORWARD.put(forward, x, 2, [ae[i, x] for i in OPPOSITE])
         return carry
 
     lax.fori_loop(0, PLANES, end_plane, 0, unroll=True)
 
-    pl.semaphore_wait(barrier, len(greeted))
+    hub_sends = len(column_hubs) - 1 + len(around) - 1
+    awaited = len(NEIGHBOURS) + jnp.where(hub, hub_sends, len(column_hubs))
+    awaited += jnp.where(first_hub, len(fourth), 0) + jnp.where(last_hub, len(third), 0)
+    pl.semaphore_wait(barrier, awaited)
     first = FORWARD.copies(forward, gx, gz, n_gx, n_gz)
-    first += BACKWARD.copies(back_mid, gx, gz, n_gx, n_gz)
     for copy in first:
         copy.start()
     for copy in first:
@@ -526,10 +558,11 @@
     def mid_plane(x, total):
         state = FORWARD.get(forward, x, 0)
         slope = FORWARD.get(forward, x, 1)
-        carried = BACKWARD.get(back_mid, x, 0)
+        mirrored = FORWARD.get(forward, x, 2)
+        carried = [mirrored[i] for i in OPPOSITE]
         adjoint, sens_mid = transposed(state, carried, por[x], kind[x])
         sens[x] = sens_mid
-        BACKWARD.put(back_start, x, 0, adjoint)
+        BACKWARD.put(back, x, 0, adjoint)
         sums = [a * b for a, b in zip(adjoint, slope)] + [sens_mid, total]
         while len(sums) > 1:
             sums = [a + b for a, b in zip(sums[::2], sums[1::2])] + sums[len(sums) & ~1 :]
@@ -551,25 +584,34 @@
         pltpu.make_async_copy(got.at[pl.ds(0, count)], got.at[pl.ds(0, count)], semaphore).wait()
 
     mine_a[...] = jnp.sum(total, axis=0, keepdims=True)
-    for target in columns:
-        reduce_copy(0, mine_a, got_a, column_at, target).start()
-    second = BACKWARD.copies(back_start, gx, gz, n_gx, n_gz)
+    for k, c in column_hubs:
+
+        @pl.when(jnp.logical_not(jnp.logical_and(hub, z == k)))
+        def _():
+            reduce_copy(0, mine_a, got_a, column_at, column(k, c)).start()
+
+    second = BACKWARD.copies(back, gx, gz, n_gx, n_gz)
     for copy in second:
         copy.start()
 
-    wait_for(red_recv.at[0], got_a, n_column - 1)
-    got_a[column_at] = mine_a[...]
-    mine_b[...] = jnp.sum(got_a[...], axis=0)
     sheet_at = x_lo * n_gz + gz
-    for target in sheets:
-        reduce_copy(1, mine_b, got_b, sheet_at, target).start()
+
+    @pl.when(hub)
+    def _():
+        wait_for(red_recv.at[0], got_a, n_column - 1)
+        got_a[column_at] = mine_a[...]
+        mine_b[...] = jnp.sum(got_a[...], axis=0)
+        each_of(
+            around, lambda target: reduce_copy(1, mine_b, got_b, sheet_at, target).start()
+        )
+        got_b[sheet_at] = mine_b[...]
 
     for copy in second:
         copy.wait_recv()
 
     def last_plane(x, carry):
         state = [cp[i, x] for i in range(CH)]
-        carried = BACKWARD.get(back_start, x, 0)
+        carried = BACKWARD.get(back, x, 0)
         adjoint, sens_start = transposed(state, carried, por[x], kind[x])
         for i in range(CH):
             out_ref[i, x] = adjoint[i]
@@ -580,11 +622,42 @@
 
     for copy in first + second:
         copy.wait_send()
-    wait_for(red_send.at[0], got_a, n_column - 1)
-    wait_for(red_send.at[1], got_b, n_sheet - 1)
-    wait_for(red_recv.at[1], got_b, n_sheet - 1)
-    got_b[sheet_at] = mine_b[...]
-    sum_ref[...] = jnp.sum(got_b[...], axis=0)
+
+    @pl.when(hub)
+    def _():
+        wait_for(red_recv.at[1], got_b, n_sheet - 1)
+
+    @pl.when(lower_only)
+    def _():
+        wait_for(red_recv.at[1], got_b, n_sheet)
+
+    @pl.when(lower)
+    def _():
+        total_row[...] = jnp.sum(got_b[...], axis=0)
+        sum_ref[...] = total_row[...]
+
+    for is_hub, targets in ((first_hub, fourth), (last_hub, third)):
+
+        @pl.when(is_hub)
+        def _():
+            for k, c in targets:
+                reduce_copy(2, total_row, got_c, 0, column(k, c)).start()
+            wait_for(red_send.at[2], got_b, len(targets))
+
+    @pl.when(upper)
+    def _():
+        wait_for(red_recv.at[2], got_c, 1)
+        sum_ref[...] = got_c[0]
+
+    @pl.when(hub)
+    def _():
+        wait_for(red_send.at[0], got_a, len(column_hubs) - 1)
+        wait_for(red_send.at[1], got_b, n_sheet - 1)
+        wait_for(red_send.at[1], got_b, n_sheet)
+
+    @pl.when(jnp.logical_not(hub))
+    def _():
+        wait_for(red_send.at[0], got_a, len(column_hubs))
 
 
 def finish(adjoint, grad, row, out_ref, grad_ref, total_ref, held, sems):
@@ -630,14 +703,15 @@
             ]
             + FORWARD.scratch()
             + BACKWARD.scratch()
-            + BACKWARD.scratch()
             + [
                 pltpu.VMEM((1, LANES), F32),
                 pltpu.VMEM((n_gx // 2, 1, LANES), F32),
                 pltpu.VMEM((1, LANES), F32),
                 pltpu.VMEM((2 * n_gz, 1, LANES), F32),
-                pltpu.SemaphoreType.DMA((2,)),
-                pltpu.SemaphoreType.DMA((2,)),
+                pltpu.VMEM((1, LANES), F32),
+                pltpu.VMEM((1, 1, LANES), F32),
+                pltpu.SemaphoreType.DMA((3,)),
+                pltpu.SemaphoreType.DMA((3,)),
             ],
             compiler_params=pltpu.CompilerParams(
                 collective_id=0, has_side_effects=True, vmem_limit_bytes=32 * 1024 * 1024

time: 31.9 us -> 30.8 us (0.966)
  Pallas kernels: 31.1 us -> 30 us
    pallas_call x1, Pallas kernels: 30.3 us -> 29.2 us  [on_device(): pl.pallas_call(lambda *refs: kernel(n_gx, n_gz, *refs), out_shape=(pltpu....]
where the time goes in v3:
time: 30.8 us; the launch traced here: 30.6 us
  Pallas kernels  30 us (97%)
  between operations  0.64 us (2%)
    pallas_call x1, Pallas kernels, on_device(): pl.pallas_call(lambda *refs: kernel(n_gx, n_gz, *refs), out_shape=(pltpu....  29.2 us
    pallas_call x1, Pallas kernels, on_device(): pl.pallas_call(finish, out_shape=(jax.ShapeDtypeStruct((CH,) + block, F32...  0.79 us

profile of v3, /device:TPU:1, one launch (start us, length us, event | category | flops | bytes accessed | tf_op | source)
XLA Modules:
  0.0 30.6 jit_solution(11170449607867377543)
XLA Ops:
  0.6 29.2 %shard_map.85 = (f32[26,4,8,128]{3,2,1,0:T(8,128)S(1)}, f32[4,8,128]{2,1,0:T(8,128)S(1)}, f32[1,128]{1,0:T(1,128)S(1)}) custom-call(f32[26,4,8,128]{3,2,1,0:T(8,128)} %refs_0_.1, f32[26,4,8,128]{3,2,1,0:T(8,128)} %refs_1_.1, f32[4,8,128]{2,1,0:T(8,128)} %refs_2_.1, s32[4,8,128]{2,1,0:T(8,128)} %refs_3_.1, s32[4,8,128]{2,1,0:T(8,128)} %refs_4_.1, f32[2]{0:T(128)} %refs_5_.1), custom_call_target="tpu_custom_call" | custom-call | tf_op jit(solution)/shard_map/pallas_call | solution.py:685
  29.8 0.8 %shard_map.86 = (f32[26,4,8,128]{3,2,1,0:T(8,128)}, f32[4,8,128]{2,1,0:T(8,128)}, f32[1,1]{1,0:T(1,128)}) custom-call(f32[26,4,8,128]{3,2,1,0:T(8,128)S(1)} %get-tuple-element.9.adjoint, f32[4,8,128]{2,1,0:T(8,128)S(1)} %get-tuple-element.10.grad, f32[1,128]{1,0:T(1,128)S(1)} %get-tuple-element.11.row), custom_call_target="tpu_custom_call" | custom-call | tf_op jit(solution)/shard_map/pallas_call | solution.py:721

commit v4 on v3

--- a/solution.py
+++ b/solution.py
@@ -440,7 +440,7 @@
     (out_ref, grad_ref, sum_ref) = refs[6:9]
     (cp, ae, por, kind, feed, conc, sens, in_sem) = refs[9:17]
     forward, back = refs[17:22], refs[22:27]
-    (mine_a, got_a, mine_b, got_b, total_row, got_c, red_send, red_recv) = refs[27:]
+    (mine_a, got_a, mine_b, got_b, total_row, got_c, got_r, red_send, red_recv) = refs[27:]
     gx, gz = lax.axis_index("gx"), lax.axis_index("gz")
     n_column, n_sheet = n_gx // 2, 2 * n_gz
     x_lo, column_at = gx // n_column, lax.rem(gx, n_column)
@@ -452,8 +452,12 @@
     upper = jnp.logical_not(lower)
     hub = jnp.logical_and(lower, core == HUB_CORE)
     lower_only = jnp.logical_and(lower, core != HUB_CORE)
-    first_hub = jnp.logical_and(hub, z == 0)
     last_hub = jnp.logical_and(hub, z == n_z // 2 - 1)
+    next_hub = jnp.logical_and(hub, z == n_z // 2 - 2)
+
+    root = jnp.logical_and(gx == HUB_CORE, gz == 0)
+    not_root = jnp.logical_not(root)
+    root_at = (HUB_CORE, 0)
 
     def column(at_z, at_core):
         return (x_lo * n_column + 2 * at_z + at_core, gz)
@@ -511,20 +515,37 @@
 
     @pl.when(upper)
     def _():
-        greet(column(jnp.where(z < 3 * n_z // 4, n_z // 2 - 1, 0), HUB_CORE))
+        greet(column(n_z // 2 - jnp.where(z < 3 * n_z // 4, 1, 2), HUB_CORE))
 
     @pl.when(lower_only)
     def _():
         for offset in to_hubs:
             greet(sheet(*offset))
 
+    @pl.when(jnp.logical_and(hub, not_root))
+    def _():
+        each_of(to_hubs, greet)
+
     @pl.when(hub)
     def _():
-        each_of(to_hubs, greet)
         greet(column(z, 1 - HUB_CORE))
         for k in range(1, n_z):
             for c in range(2):
                 greet(column(lax.rem(z + k, n_z), c))
+
+    @pl.when(root)
+    def _():
+        @pl.loop(0, n_gx)
+        def _(k):
+            to_gx = lax.rem(k, 2) * n_column + n_column - 1 - k // 2
+            for to_gz in range(n_gz):
+                if to_gz:
+                    greet((to_gx, to_gz))
+                else:
+
+                    @pl.when(to_gx != HUB_CORE)
+                    def _():
+                        greet((to_gx, to_gz))
 
     for load in loads[:5]:
         load.wait()
@@ -547,7 +568,8 @@
 
     hub_sends = len(column_hubs) - 1 + len(around) - 1
     awaited = len(NEIGHBOURS) + jnp.where(hub, hub_sends, len(column_hubs))
-    awaited += jnp.where(first_hub, len(fourth), 0) + jnp.where(last_hub, len(third), 0)
+    awaited += jnp.where(root, 0, 1) - jnp.where(jnp.logical_and(jnp.logical_and(hub, z == 0), not_root), 1, 0)
+    awaited += jnp.where(next_hub, len(fourth), 0) + jnp.where(last_hub, len(third), 0)
     pl.semaphore_wait(barrier, awaited)
     first = FORWARD.copies(forward, gx, gz, n_gx, n_gz)
     for copy in first:
@@ -584,6 +606,10 @@
         pltpu.make_async_copy(got.at[pl.ds(0, count)], got.at[pl.ds(0, count)], semaphore).wait()
 
     mine_a[...] = jnp.sum(total, axis=0, keepdims=True)
+    @pl.when(not_root)
+    def _():
+        reduce_copy(3, mine_a, got_r, pl.ds(gx * n_gz + gz, 1), root_at).start()
+
     for k, c in column_hubs:
 
         @pl.when(jnp.logical_not(jnp.logical_and(hub, z == k)))
@@ -596,14 +622,19 @@
 
     sheet_at = x_lo * n_gz + gz
 
+    def send_sheet(target):
+        copy = reduce_copy(1, mine_b, got_b, sheet_at, target)
+
+        @pl.when(jnp.logical_or(target[0] != HUB_CORE, target[1] != 0))
+        def _():
+            copy.start()
+
     @pl.when(hub)
     def _():
         wait_for(red_recv.at[0], got_a, n_column - 1)
         got_a[column_at] = mine_a[...]
         mine_b[...] = jnp.sum(got_a[...], axis=0)
-        each_of(
-            around, lambda target: reduce_copy(1, mine_b, got_b, sheet_at, target).start()
-        )
+        each_of(around, send_sheet)
         got_b[sheet_at] = mine_b[...]
 
     for copy in second:
@@ -623,7 +654,7 @@
     for copy in first + second:
         copy.wait_send()
 
-    @pl.when(hub)
+    @pl.when(jnp.logical_and(hub, not_root))
     def _():
         wait_for(red_recv.at[1], got_b, n_sheet - 1)
 
@@ -631,12 +662,19 @@
     def _():
         wait_for(red_recv.at[1], got_b, n_sheet)
 
-    @pl.when(lower)
+    @pl.when(jnp.logical_and(lower, not_root))
     def _():
         total_row[...] = jnp.sum(got_b[...], axis=0)
         sum_ref[...] = total_row[...]
 
-    for is_hub, targets in ((first_hub, fourth), (last_hub, third)):
+    @pl.when(root)
+    def _():
+        wait_for(red_recv.at[3], got_r, n_gx * n_gz - 1)
+        got_r[pl.ds(HUB_CORE * n_gz, 1), :] = mine_a[...]
+        total_row[...] = jnp.sum(got_r[...], axis=0, keepdims=True)
+        sum_ref[...] = total_row[...]
+
+    for is_hub, targets in ((next_hub, fourth), (last_hub, third)):
 
         @pl.when(is_hub)
         def _():
@@ -652,8 +690,16 @@
     @pl.when(hub)
     def _():
         wait_for(red_send.at[0], got_a, len(column_hubs) - 1)
-        wait_for(red_send.at[1], got_b, n_sheet - 1)
+        wait_for(red_send.at[1], got_b, n_sheet - 2)
         wait_for(red_send.at[1], got_b, n_sheet)
+
+    @pl.when(jnp.logical_and(hub, jnp.logical_or(root, z != 0)))
+    def _():
+        wait_for(red_send.at[1], got_b, 1)
+
+    @pl.when(not_root)
+    def _():
+        wait_for(red_send.at[3], got_r, 1)
 
     @pl.when(jnp.logical_not(hub))
     def _():
@@ -710,8 +756,9 @@
                 pltpu.VMEM((2 * n_gz, 1, LANES), F32),
                 pltpu.VMEM((1, LANES), F32),
                 pltpu.VMEM((1, 1, LANES), F32),
-                pltpu.SemaphoreType.DMA((3,)),
-                pltpu.SemaphoreType.DMA((3,)),
+                pltpu.VMEM((n_gx * n_gz, LANES), F32),
+                pltpu.SemaphoreType.DMA((4,)),
+                pltpu.SemaphoreType.DMA((4,)),
             ],
             compiler_params=pltpu.CompilerParams(
                 collective_id=0, has_side_effects=True, vmem_limit_bytes=32 * 1024 * 1024

time: 30.8 us -> 29 us (0.942)
  Pallas kernels: 30 us -> 27.9 us
    pallas_call x1, Pallas kernels: 29.2 us -> 27.1 us  [on_device(): pl.pallas_call(lambda *refs: kernel(n_gx, n_gz, *refs), out_shape=(pltpu....]
where the time goes in v4:
time: 29 us; the launch traced here: 28.6 us
  Pallas kernels  27.9 us (96%)
  between operations  0.64 us (2%)
    pallas_call x1, Pallas kernels, on_device(): pl.pallas_call(lambda *refs: kernel(n_gx, n_gz, *refs), out_shape=(pltpu....  27.1 us
    pallas_call x1, Pallas kernels, on_device(): pl.pallas_call(finish, out_shape=(jax.ShapeDtypeStruct((CH,) + block, F32...  0.79 us

profile of v4, /device:TPU:1, one launch (start us, length us, event | category | flops | bytes accessed | tf_op | source)
XLA Modules:
  0.0 28.6 jit_solution(12356695316096437910)
XLA Ops:
  0.6 27.1 %shard_map.85 = (f32[26,4,8,128]{3,2,1,0:T(8,128)S(1)}, f32[4,8,128]{2,1,0:T(8,128)S(1)}, f32[1,128]{1,0:T(1,128)S(1)}) custom-call(f32[26,4,8,128]{3,2,1,0:T(8,128)} %refs_0_.1, f32[26,4,8,128]{3,2,1,0:T(8,128)} %refs_1_.1, f32[4,8,128]{2,1,0:T(8,128)} %refs_2_.1, s32[4,8,128]{2,1,0:T(8,128)} %refs_3_.1, s32[4,8,128]{2,1,0:T(8,128)} %refs_4_.1, f32[2]{0:T(128)} %refs_5_.1), custom_call_target="tpu_custom_call" | custom-call | tf_op jit(solution)/shard_map/pallas_call | solution.py:731
  27.8 0.8 %shard_map.86 = (f32[26,4,8,128]{3,2,1,0:T(8,128)}, f32[4,8,128]{2,1,0:T(8,128)}, f32[1,1]{1,0:T(1,128)}) custom-call(f32[26,4,8,128]{3,2,1,0:T(8,128)S(1)} %get-tuple-element.9.adjoint, f32[4,8,128]{2,1,0:T(8,128)S(1)} %get-tuple-element.10.grad, f32[1,128]{1,0:T(1,128)S(1)} %get-tuple-element.11.row), custom_call_target="tpu_custom_call" | custom-call | tf_op jit(solution)/shard_map/pallas_call | solution.py:768

commit v5 on v4

--- a/solution.py
+++ b/solution.py
@@ -35,7 +35,7 @@
 ROWS = 8
 LANES = 128
 
-NEIGHBOURS = ((1, 1), (1, -1), (-1, 1), (-1, -1), (0, 1), (0, -1), (1, 0), (-1, 0))
+NEIGHBOURS = ((1, 0), (-1, 0), (1, 1), (1, -1), (-1, 1), (-1, -1), (0, 1), (0, -1))
 
 HUB_CORE = 1
 
@@ -574,9 +574,6 @@
     first = FORWARD.copies(forward, gx, gz, n_gx, n_gz)
     for copy in first:
         copy.start()
-    for copy in first:
-        copy.wait_recv()
-
     def mid_plane(x, total):
         state = FORWARD.get(forward, x, 0)
         slope = FORWARD.get(forward, x, 1)
@@ -590,7 +587,15 @@
             sums = [a + b for a, b in zip(sums[::2], sums[1::2])] + sums[len(sums) & ~1 :]
         return sums[0]
 
-    total = lax.fori_loop(0, PLANES, mid_plane, jnp.zeros((ROWS, LANES), F32), unroll=True)
+    over_z = [copy for copy, (dx, dz) in zip(first, NEIGHBOURS) if dx == 0]
+    over_x = [copy for copy, (dx, dz) in zip(first, NEIGHBOURS) if dx != 0]
+    for copy in over_z:
+        copy.wait_recv()
+    total = jnp.zeros((ROWS, LANES), F32)
+    total = lax.fori_loop(0, PLANES - 2, lambda k, t: mid_plane(k + 1, t), total, unroll=True)
+    for copy in over_x:
+        copy.wait_recv()
+    total = lax.fori_loop(0, 2, lambda k, t: mid_plane(k * (PLANES - 1), t), total, unroll=True)
 
     def reduce_copy(stage, mine, got, slot, target):
         return pltpu.make_async_remote_copy(
@@ -605,10 +610,18 @@
     def wait_for(semaphore, got, count):
         pltpu.make_async_copy(got.at[pl.ds(0, count)], got.at[pl.ds(0, count)], semaphore).wait()
 
+    def in_order(terms):
+        sum_of = terms[0]
+        for term in terms[1:]:
+            sum_of = sum_of + term
+        return sum_of
+
     mine_a[...] = jnp.sum(total, axis=0, keepdims=True)
+    sheet_at = x_lo * n_gz + gz
+
     @pl.when(not_root)
     def _():
-        reduce_copy(3, mine_a, got_r, pl.ds(gx * n_gz + gz, 1), root_at).start()
+        reduce_copy(3, mine_a, got_r, pl.ds(column_at * n_sheet + sheet_at, 1), root_at).start()
 
     for k, c in column_hubs:
 
@@ -620,22 +633,23 @@
     for copy in second:
         copy.start()
 
-    sheet_at = x_lo * n_gz + gz
-
     def send_sheet(target):
-        copy = reduce_copy(1, mine_b, got_b, sheet_at, target)
-
+        reduce_copy(1, mine_b, got_b, pl.ds(sheet_at, 1), target).start()
+
+    def send_unless_root(target):
         @pl.when(jnp.logical_or(target[0] != HUB_CORE, target[1] != 0))
         def _():
-            copy.start()
+            send_sheet(target)
 
     @pl.when(hub)
     def _():
         wait_for(red_recv.at[0], got_a, n_column - 1)
         got_a[column_at] = mine_a[...]
-        mine_b[...] = jnp.sum(got_a[...], axis=0)
-        each_of(around, send_sheet)
-        got_b[sheet_at] = mine_b[...]
+        mine_b[...] = in_order([got_a[k] for k in range(n_column)])
+        may_be_root = [o for o in around if o[2] == 0 and o[3] == HUB_CORE]
+        each_of([o for o in around if o not in may_be_root], send_sheet)
+        each_of(may_be_root, send_unless_root)
+        got_b[pl.ds(sheet_at, 1), :] = mine_b[...]
 
     for copy in second:
         copy.wait_recv()
@@ -664,14 +678,15 @@
 
     @pl.when(jnp.logical_and(lower, not_root))
     def _():
-        total_row[...] = jnp.sum(got_b[...], axis=0)
+        total_row[...] = jnp.sum(got_b[...], axis=0, keepdims=True)
         sum_ref[...] = total_row[...]
 
     @pl.when(root)
     def _():
-        wait_for(red_recv.at[3], got_r, n_gx * n_gz - 1)
-        got_r[pl.ds(HUB_CORE * n_gz, 1), :] = mine_a[...]
-        total_row[...] = jnp.sum(got_r[...], axis=0, keepdims=True)
+        wait_for(red_recv.at[3], got_r, n_column * n_sheet - 1)
+        got_r[pl.ds(HUB_CORE * n_sheet, 1), :] = mine_a[...]
+        sheet_sums = in_order([got_r[pl.ds(k * n_sheet, n_sheet), :] for k in range(n_column)])
+        total_row[...] = jnp.sum(sheet_sums, axis=0, keepdims=True)
         sum_ref[...] = total_row[...]
 
     for is_hub, targets in ((next_hub, fourth), (last_hub, third)):
@@ -699,7 +714,7 @@
 
     @pl.when(not_root)
     def _():
-        wait_for(red_send.at[3], got_r, 1)
+        wait_for(red_send.at[3], got_b, 1)
 
     @pl.when(jnp.logical_not(hub))
     def _():
@@ -753,7 +768,7 @@
                 pltpu.VMEM((1, LANES), F32),
                 pltpu.VMEM((n_gx // 2, 1, LANES), F32),
                 pltpu.VMEM((1, LANES), F32),
-                pltpu.VMEM((2 * n_gz, 1, LANES), F32),
+                pltpu.VMEM((2 * n_gz, LANES), F32),
                 pltpu.VMEM((1, LANES), F32),
                 pltpu.VMEM((1, 1, LANES), F32),
                 pltpu.VMEM((n_gx * n_gz, LANES), F32),

time: 29 us -> 28.8 us (level)
  no operation moved by 1% of the time
where the time goes in v5:
time: 28.8 us; the launch traced here: 28.4 us
  Pallas kernels  27.7 us (96%)
  between operations  0.64 us (2%)
    pallas_call x1, Pallas kernels, on_device(): pl.pallas_call(lambda *refs: kernel(n_gx, n_gz, *refs), out_shape=(pltpu....  27 us
    pallas_call x1, Pallas kernels, on_device(): pl.pallas_call(finish, out_shape=(jax.ShapeDtypeStruct((CH,) + block, F32...  0.79 us

profile of v5, /device:TPU:1, one launch (start us, length us, event | category | flops | bytes accessed | tf_op | source)
XLA Modules:
  0.0 28.4 jit_solution(13014820672785767072)
XLA Ops:
  0.6 27.0 %shard_map.85 = (f32[26,4,8,128]{3,2,1,0:T(8,128)S(1)}, f32[4,8,128]{2,1,0:T(8,128)S(1)}, f32[1,128]{1,0:T(1,128)S(1)}) custom-call(f32[26,4,8,128]{3,2,1,0:T(8,128)} %refs_0_.1, f32[26,4,8,128]{3,2,1,0:T(8,128)} %refs_1_.1, f32[4,8,128]{2,1,0:T(8,128)} %refs_2_.1, s32[4,8,128]{2,1,0:T(8,128)} %refs_3_.1, s32[4,8,128]{2,1,0:T(8,128)} %refs_4_.1, f32[2]{0:T(128)} %refs_5_.1), custom_call_target="tpu_custom_call" | custom-call | tf_op jit(solution)/shard_map/pallas_call | solution.py:746
  27.6 0.8 %shard_map.86 = (f32[26,4,8,128]{3,2,1,0:T(8,128)}, f32[4,8,128]{2,1,0:T(8,128)}, f32[1,1]{1,0:T(1,128)}) custom-call(f32[26,4,8,128]{3,2,1,0:T(8,128)S(1)} %get-tuple-element.9.adjoint, f32[4,8,128]{2,1,0:T(8,128)S(1)} %get-tuple-element.10.grad, f32[1,128]{1,0:T(1,128)S(1)} %get-tuple-element.11.row), custom_call_target="tpu_custom_call" | custom-call | tf_op jit(solution)/shard_map/pallas_call | solution.py:783

commit v6 on v5

--- a/solution.py
+++ b/solution.py
@@ -357,6 +357,8 @@
             group.sort(key=lambda i: -abs(self.vel[i][0]))
             keys = [(k, i) for i in group for k in range(fields)]
             self.z_count = len(keys)
+            self.rows_over_z = 2 * self.z_count * PLANES
+            self.rows_over_x = 2 * self.face * ROWS + 4 * fields
             for at, key in enumerate(keys):
                 self.z_place[key] = (0 if sign == 1 else 1, at)
             for at, i in enumerate(group[:2]):
@@ -367,8 +369,8 @@
             pltpu.VMEM((CH * self.fields, PLANES + 2, ROWS, LANES), F32),
             pltpu.VMEM((2, self.z_count, PLANES, 1, LANES), F32),
             pltpu.VMEM((2, self.z_count, PLANES + 2, 1, LANES), F32),
-            pltpu.SemaphoreType.DMA((8,)),
-            pltpu.SemaphoreType.DMA((8,)),
+            pltpu.SemaphoreType.DMA((1,)),
+            pltpu.SemaphoreType.DMA((2,)),
         ]
 
     def put(self, refs, x, field, values):
@@ -386,7 +388,7 @@
     def copies(self, refs, gx, gz, n_gx, n_gz):
         padded, rows, halo, send, recv = refs
         found = []
-        for at, (dx, dz) in enumerate(NEIGHBOURS):
+        for dx, dz in NEIGHBOURS:
             target = (lax.rem(gx + dx + n_gx, n_gx), lax.rem(gz + dz + n_gz, n_gz))
             side = 0 if dz == 1 else 1
             if dz == 0:
@@ -404,8 +406,8 @@
                 pltpu.make_async_remote_copy(
                     src_ref=source,
                     dst_ref=landing,
-                    send_sem=send.at[at],
-                    recv_sem=recv.at[at],
+                    send_sem=send.at[0],
+                    recv_sem=recv.at[0 if dx == 0 else 1],
                     device_id=target,
                     device_id_type=MESH,
                 )
@@ -499,15 +501,13 @@
 
     loads = [
         pltpu.make_async_copy(source, target, in_sem.at[k])
-        for k, (source, target) in enumerate(
-            (
-                (checkpoint, cp),
-                (porosity, por),
-                (node_type, kind),
-                (inlet_index, feed),
-                (inlet_conc, conc),
-                (adjoint_end, ae),
-            )
+        for source, target, k in (
+            (checkpoint, cp, 0),
+            (porosity, por, 0),
+            (node_type, kind, 0),
+            (inlet_index, feed, 0),
+            (inlet_conc, conc, 1),
+            (adjoint_end, ae, 2),
         )
     ]
     for load in loads:
@@ -547,8 +547,9 @@
                     def _():
                         greet((to_gx, to_gz))
 
-    for load in loads[:5]:
-        load.wait()
+    loaded = forward[0].at[pl.ds(0, CH + 3), pl.ds(0, PLANES)]
+    pltpu.make_async_copy(loaded, loaded, in_sem.at[0]).wait()
+    loads[4].wait()
 
     def start_plane(x, carry):
         level = jnp.where(feed[x] == 0, conc[0], jnp.where(feed[x] == 1, conc[1], 0.0))
@@ -571,8 +572,7 @@
     awaited += jnp.where(root, 0, 1) - jnp.where(jnp.logical_and(jnp.logical_and(hub, z == 0), not_root), 1, 0)
     awaited += jnp.where(next_hub, len(fourth), 0) + jnp.where(last_hub, len(third), 0)
     pl.semaphore_wait(barrier, awaited)
-    first = FORWARD.copies(forward, gx, gz, n_gx, n_gz)
-    for copy in first:
+    for copy in FORWARD.copies(forward, gx, gz, n_gx, n_gz):
         copy.start()
     def mid_plane(x, total):
         state = FORWARD.get(forward, x, 0)
@@ -587,28 +587,24 @@
             sums = [a + b for a, b in zip(sums[::2], sums[1::2])] + sums[len(sums) & ~1 :]
         return sums[0]
 
-    over_z = [copy for copy, (dx, dz) in zip(first, NEIGHBOURS) if dx == 0]
-    over_x = [copy for copy, (dx, dz) in zip(first, NEIGHBOURS) if dx != 0]
-    for copy in over_z:
-        copy.wait_recv()
+    def wait_for(semaphore, got, count):
+        pltpu.make_async_copy(got.at[pl.ds(0, count)], got.at[pl.ds(0, count)], semaphore).wait()
+
+    wait_for(forward[4].at[0], got_r, FORWARD.rows_over_z)
     total = jnp.zeros((ROWS, LANES), F32)
     total = lax.fori_loop(0, PLANES - 2, lambda k, t: mid_plane(k + 1, t), total, unroll=True)
-    for copy in over_x:
-        copy.wait_recv()
+    wait_for(forward[4].at[1], got_r, FORWARD.rows_over_x)
     total = lax.fori_loop(0, 2, lambda k, t: mid_plane(k * (PLANES - 1), t), total, unroll=True)
 
     def reduce_copy(stage, mine, got, slot, target):
         return pltpu.make_async_remote_copy(
             src_ref=mine,
             dst_ref=got.at[slot],
-            send_sem=red_send.at[stage],
-            recv_sem=red_recv.at[stage],
+            send_sem=red_send.at[0],
+            recv_sem=red_recv.at[min(stage, 1)],
             device_id=target,
             device_id_type=MESH,
         )
-
-    def wait_for(semaphore, got, count):
-        pltpu.make_async_copy(got.at[pl.ds(0, count)], got.at[pl.ds(0, count)], semaphore).wait()
 
     def in_order(terms):
         sum_of = terms[0]
@@ -629,8 +625,7 @@
         def _():
             reduce_copy(0, mine_a, got_a, column_at, column(k, c)).start()
 
-    second = BACKWARD.copies(back, gx, gz, n_gx, n_gz)
-    for copy in second:
+    for copy in BACKWARD.copies(back, gx, gz, n_gx, n_gz):
         copy.start()
 
     def send_sheet(target):
@@ -651,8 +646,8 @@
         each_of(may_be_root, send_unless_root)
         got_b[pl.ds(sheet_at, 1), :] = mine_b[...]
 
-    for copy in second:
-        copy.wait_recv()
+    wait_for(back[4].at[0], got_r, BACKWARD.rows_over_z)
+    wait_for(back[4].at[1], got_r, BACKWARD.rows_over_x)
 
     def last_plane(x, carry):
         state = [cp[i, x] for i in range(CH)]
@@ -665,8 +660,8 @@
 
     lax.fori_loop(0, PLANES, last_plane, 0, unroll=True)
 
-    for copy in first + second:
-        copy.wait_send()
+    wait_for(forward[3].at[0], got_r, FORWARD.rows_over_z + FORWARD.rows_over_x)
+    wait_for(back[3].at[0], got_r, BACKWARD.rows_over_z + BACKWARD.rows_over_x)
 
     @pl.when(jnp.logical_and(hub, not_root))
     def _():
@@ -683,7 +678,7 @@
 
     @pl.when(root)
     def _():
-        wait_for(red_recv.at[3], got_r, n_column * n_sheet - 1)
+        wait_for(red_recv.at[1], got_r, n_column * n_sheet - 1)
         got_r[pl.ds(HUB_CORE * n_sheet, 1), :] = mine_a[...]
         sheet_sums = in_order([got_r[pl.ds(k * n_sheet, n_sheet), :] for k in range(n_column)])
         total_row[...] = jnp.sum(sheet_sums, axis=0, keepdims=True)
@@ -695,30 +690,24 @@
         def _():
             for k, c in targets:
                 reduce_copy(2, total_row, got_c, 0, column(k, c)).start()
-            wait_for(red_send.at[2], got_b, len(targets))
 
     @pl.when(upper)
     def _():
-        wait_for(red_recv.at[2], got_c, 1)
+        wait_for(red_recv.at[1], got_c, 1)
         sum_ref[...] = got_c[0]
 
-    @pl.when(hub)
-    def _():
-        wait_for(red_send.at[0], got_a, len(column_hubs) - 1)
-        wait_for(red_send.at[1], got_b, n_sheet - 2)
-        wait_for(red_send.at[1], got_b, n_sheet)
-
-    @pl.when(jnp.logical_and(hub, jnp.logical_or(root, z != 0)))
-    def _():
-        wait_for(red_send.at[1], got_b, 1)
-
-    @pl.when(not_root)
-    def _():
-        wait_for(red_send.at[3], got_b, 1)
-
-    @pl.when(jnp.logical_not(hub))
-    def _():
-        wait_for(red_send.at[0], got_a, len(column_hubs))
+    hub_rows = len(column_hubs) - 1 + len(around) - 1
+    for kind_of, rows_sent in (
+        (jnp.logical_not(hub), len(column_hubs) + 1),
+        (jnp.logical_and(hub, z == 0), hub_rows),
+        (next_hub, hub_rows + 1 + len(fourth)),
+        (last_hub, hub_rows + 1 + len(third)),
+        (jnp.logical_and(hub, jnp.logical_and(z > 0, z < n_z // 2 - 2)), hub_rows + 1),
+    ):
+
+        @pl.when(kind_of)
+        def _():
+            wait_for(red_send.at[0], got_r, rows_sent)
 
 
 def finish(adjoint, grad, row, out_ref, grad_ref, total_ref, held, sems):
@@ -760,7 +749,7 @@
                 pltpu.VMEM(block, jnp.int32),
                 pltpu.SMEM((2,), F32),
                 pltpu.VMEM(block, F32),
-                pltpu.SemaphoreType.DMA((6,)),
+                pltpu.SemaphoreType.DMA((3,)),
             ]
             + FORWARD.scratch()
             + BACKWARD.scratch()
@@ -772,8 +761,8 @@
                 pltpu.VMEM((1, LANES), F32),
                 pltpu.VMEM((1, 1, LANES), F32),
                 pltpu.VMEM((n_gx * n_gz, LANES), F32),
-                pltpu.SemaphoreType.DMA((4,)),
-                pltpu.SemaphoreType.DMA((4,)),
+                pltpu.SemaphoreType.DMA((1,)),
+                pltpu.SemaphoreType.DMA((2,)),
             ],
             compiler_params=pltpu.CompilerParams(
                 collective_id=0, has_side_effects=True, vmem_limit_bytes=32 * 1024 * 1024

time: 28.8 us -> 28.5 us (0.990)
  Pallas kernels: 27.7 us -> 27.4 us
    pallas_call x1, Pallas kernels: 27 us -> 26.7 us  [on_device(): pl.pallas_call(lambda *refs: kernel(n_gx, n_gz, *refs), out_shape=(pltpu....]
where the time goes in v6:
time: 28.5 us; the launch traced here: 28.1 us
  Pallas kernels  27.4 us (96%)
  between operations  0.64 us (2%)
    pallas_call x1, Pallas kernels, on_device(): pl.pallas_call(lambda *refs: kernel(n_gx, n_gz, *refs), out_shape=(pltpu....  26.7 us
    pallas_call x1, Pallas kernels, on_device(): pl.pallas_call(finish, out_shape=(jax.ShapeDtypeStruct((CH,) + block, F32...  0.79 us

profile of v6, /device:TPU:1, one launch (start us, length us, event | category | flops | bytes accessed | tf_op | source)
XLA Modules:
  0.0 28.1 jit_solution(18365492206578719284)
XLA Ops:
  0.6 26.7 %shard_map.85 = (f32[26,4,8,128]{3,2,1,0:T(8,128)S(1)}, f32[4,8,128]{2,1,0:T(8,128)S(1)}, f32[1,128]{1,0:T(1,128)S(1)}) custom-call(f32[26,4,8,128]{3,2,1,0:T(8,128)} %refs_0_.1, f32[26,4,8,128]{3,2,1,0:T(8,128)} %refs_1_.1, f32[4,8,128]{2,1,0:T(8,128)} %refs_2_.1, s32[4,8,128]{2,1,0:T(8,128)} %refs_3_.1, s32[4,8,128]{2,1,0:T(8,128)} %refs_4_.1, f32[2]{0:T(128)} %refs_5_.1), custom_call_target="tpu_custom_call" | custom-call | tf_op jit(solution)/shard_map/pallas_call | solution.py:735
  27.3 0.8 %shard_map.86 = (f32[26,4,8,128]{3,2,1,0:T(8,128)}, f32[4,8,128]{2,1,0:T(8,128)}, f32[1,1]{1,0:T(1,128)}) custom-call(f32[26,4,8,128]{3,2,1,0:T(8,128)S(1)} %get-tuple-element.9.adjoint, f32[4,8,128]{2,1,0:T(8,128)S(1)} %get-tuple-element.10.grad, f32[1,128]{1,0:T(1,128)S(1)} %get-tuple-element.11.row), custom_call_target="tpu_custom_call" | custom-call | tf_op jit(solution)/shard_map/pallas_call | solution.py:772

commit v7 on v6

--- a/solution.py
+++ b/solution.py
@@ -466,20 +466,26 @@
 
     n_y = n_gz // 2
 
+    sheet_at = x_lo * n_gz + gz
+
     def sheet(lo, hi, at_y, at_core):
-        to_gz = lax.rem(x_hi + hi, 2) * n_y + at_y
-        return (lax.rem(x_lo + lo, 2) * n_column + 2 * z + at_core, to_gz)
-
-    rows = [*reversed(range(n_y // 2)), *reversed(range(n_y // 2, n_y))]
-    around = [(lo, hi, k, c) for k in rows for hi in (1, 0) for lo in (1, 0) for c in (1 - HUB_CORE, HUB_CORE)]
+        return (lo * n_column + 2 * z + at_core, hi * n_y + at_y)
+
+    around = [
+        (lo, hi, k, c)
+        for half in range(2)
+        for lo, hi in ((0, 0), (1, 0), (1, 1), (0, 1))
+        for k in reversed(range(half * n_y // 2, (half + 1) * n_y // 2))
+        for c in (1 - HUB_CORE, HUB_CORE)
+    ]
 
     def each_of(offsets, act):
         for lo, hi, k, c in offsets:
-            if lo or hi or c != HUB_CORE:
+            if c != HUB_CORE:
                 act(sheet(lo, hi, k, c))
             else:
 
-                @pl.when(y != k)
+                @pl.when(sheet_at != lo * n_gz + hi * n_y + k)
                 def _():
                     act(sheet(lo, hi, k, c))
 
@@ -613,7 +619,6 @@
         return sum_of
 
     mine_a[...] = jnp.sum(total, axis=0, keepdims=True)
-    sheet_at = x_lo * n_gz + gz
 
     @pl.when(not_root)
     def _():
@@ -641,7 +646,7 @@
         wait_for(red_recv.at[0], got_a, n_column - 1)
         got_a[column_at] = mine_a[...]
         mine_b[...] = in_order([got_a[k] for k in range(n_column)])
-        may_be_root = [o for o in around if o[2] == 0 and o[3] == HUB_CORE]
+        may_be_root = [(0, 0, 0, HUB_CORE)]
         each_of([o for o in around if o not in may_be_root], send_sheet)
         each_of(may_be_root, send_unless_root)
         got_b[pl.ds(sheet_at, 1), :] = mine_b[...]

time: 28.5 us -> 28.4 us (level)
  no operation moved by 1% of the time
where the time goes in v7:
time: 28.4 us; the launch traced here: 28.1 us
  Pallas kernels  27.4 us (96%)
  between operations  0.64 us (2%)
    pallas_call x1, Pallas kernels, on_device(): pl.pallas_call(lambda *refs: kernel(n_gx, n_gz, *refs), out_shape=(pltpu....  26.6 us
    pallas_call x1, Pallas kernels, on_device(): pl.pallas_call(finish, out_shape=(jax.ShapeDtypeStruct((CH,) + block, F32...  0.79 us

profile of v7, /device:TPU:1, one launch (start us, length us, event | category | flops | bytes accessed | tf_op | source)
XLA Modules:
  0.0 28.1 jit_solution(229197305152808262)
XLA Ops:
  0.6 26.6 %shard_map.85 = (f32[26,4,8,128]{3,2,1,0:T(8,128)S(1)}, f32[4,8,128]{2,1,0:T(8,128)S(1)}, f32[1,128]{1,0:T(1,128)S(1)}) custom-call(f32[26,4,8,128]{3,2,1,0:T(8,128)} %refs_0_.1, f32[26,4,8,128]{3,2,1,0:T(8,128)} %refs_1_.1, f32[4,8,128]{2,1,0:T(8,128)} %refs_2_.1, s32[4,8,128]{2,1,0:T(8,128)} %refs_3_.1, s32[4,8,128]{2,1,0:T(8,128)} %refs_4_.1, f32[2]{0:T(128)} %refs_5_.1), custom_call_target="tpu_custom_call" | custom-call | tf_op jit(solution)/shard_map/pallas_call | solution.py:740
  27.3 0.8 %shard_map.86 = (f32[26,4,8,128]{3,2,1,0:T(8,128)}, f32[4,8,128]{2,1,0:T(8,128)}, f32[1,1]{1,0:T(1,128)}) custom-call(f32[26,4,8,128]{3,2,1,0:T(8,128)S(1)} %get-tuple-element.9.adjoint, f32[4,8,128]{2,1,0:T(8,128)S(1)} %get-tuple-element.10.grad, f32[1,128]{1,0:T(1,128)S(1)} %get-tuple-element.11.row), custom_call_target="tpu_custom_call" | custom-call | tf_op jit(solution)/shard_map/pallas_call | solution.py:777

commit v8 on v7

--- a/solution.py
+++ b/solution.py
@@ -587,7 +587,8 @@
         carried = [mirrored[i] for i in OPPOSITE]
         adjoint, sens_mid = transposed(state, carried, por[x], kind[x])
         sens[x] = sens_mid
-        BACKWARD.put(back, x, 0, adjoint)
+        for i in range(CH):
+            ae[i, x] = adjoint[i]
         sums = [a * b for a, b in zip(adjoint, slope)] + [sens_mid, total]
         while len(sums) > 1:
             sums = [a + b for a, b in zip(sums[::2], sums[1::2])] + sums[len(sums) & ~1 :]
@@ -630,6 +631,11 @@
         def _():
             reduce_copy(0, mine_a, got_a, column_at, column(k, c)).start()
 
+    def back_plane(x, carry):
+        BACKWARD.put(back, x, 0, [ae[i, x] for i in range(CH)])
+        return carry
+
+    lax.fori_loop(0, PLANES, back_plane, 0, unroll=True)
     for copy in BACKWARD.copies(back, gx, gz, n_gx, n_gz):
         copy.start()
 

time: 28.4 us -> 28.4 us (level)
  no operation moved by 1% of the time
where the time goes in v8:
time: 28.4 us; the launch traced here: 28 us
  Pallas kernels  27.4 us (96%)
  between operations  0.64 us (2%)
    pallas_call x1, Pallas kernels, on_device(): pl.pallas_call(lambda *refs: kernel(n_gx, n_gz, *refs), out_shape=(pltpu....  26.6 us
    pallas_call x1, Pallas kernels, on_device(): pl.pallas_call(finish, out_shape=(jax.ShapeDtypeStruct((CH,) + block, F32...  0.79 us

profile of v8, /device:TPU:1, one launch (start us, length us, event | category | flops | bytes accessed | tf_op | source)
XLA Modules:
  0.0 28.0 jit_solution(4100296952557963433)
XLA Ops:
  0.6 26.6 %shard_map.85 = (f32[26,4,8,128]{3,2,1,0:T(8,128)S(1)}, f32[4,8,128]{2,1,0:T(8,128)S(1)}, f32[1,128]{1,0:T(1,128)S(1)}) custom-call(f32[26,4,8,128]{3,2,1,0:T(8,128)} %refs_0_.1, f32[26,4,8,128]{3,2,1,0:T(8,128)} %refs_1_.1, f32[4,8,128]{2,1,0:T(8,128)} %refs_2_.1, s32[4,8,128]{2,1,0:T(8,128)} %refs_3_.1, s32[4,8,128]{2,1,0:T(8,128)} %refs_4_.1, f32[2]{0:T(128)} %refs_5_.1), custom_call_target="tpu_custom_call" | custom-call | tf_op jit(solution)/shard_map/pallas_call | solution.py:746
  27.2 0.8 %shard_map.86 = (f32[26,4,8,128]{3,2,1,0:T(8,128)}, f32[4,8,128]{2,1,0:T(8,128)}, f32[1,1]{1,0:T(1,128)}) custom-call(f32[26,4,8,128]{3,2,1,0:T(8,128)S(1)} %get-tuple-element.9.adjoint, f32[4,8,128]{2,1,0:T(8,128)S(1)} %get-tuple-element.10.grad, f32[1,128]{1,0:T(1,128)S(1)} %get-tuple-element.11.row), custom_call_target="tpu_custom_call" | custom-call | tf_op jit(solution)/shard_map/pallas_call | solution.py:783
